TPU v7x, 32 devices: a whole 2x2x4 slice. The times are simulated.
32 devices in a mesh: px: 4 (over z), py: 8 (over y, x, core).
Axes of the slice: x: 2, y: 2, z: 4, core: 2. Of those that a mesh axis runs over, the one named last changes fastest.
Arguments:
- a_blocks: bfloat16 [3072, 27, 4096], P(('px', 'py')), may hold values from -1.5 to 1.5
- p_blocks: bfloat16 [3072, 4096], P(('px', 'py')), may hold values from -0.75 to 0.75
- a_source: int32 [3072, 27], P(('px', 'py')), may hold values from 0 to 351, as said below
- send_list: int32 [32, 32, 8], P(('px', 'py')), may hold values from -1 to 95, as said below
- agg_local: int32 [3072], P(('px', 'py')), may hold values from 0 to 15, as said below
- coarse_slot: int32 [3072, 27], P(('px', 'py')), may hold values from 0 to 26
- coarse_target: int32 [512], P(('px', 'py')), may hold values from 0 to 511, as said below
Outputs:
- coarse: bfloat16 [512, 27, 4096], P(('px', 'py'))
Inputs may be any that keep to these rules, and one draw needn't show every extreme that they name: `a_source`: column 0 of a row is the row itself. An entry of 96 or more names a slot received from device (entry - 96) // 8, slot (entry - 96) % 8, which that device fills; every filled slot is named by some entry of the receiving device. `send_list`: filled slots from one sender to one receiver come first; no device sends to itself; each device fills all 8 slots for the device after it in px+py order; row 95 is sent in every draw. `agg_local`: each of a device's 16 agglomerates holds exactly 6 of its elements. `coarse_target`: A permutation of the coarse rows; the rows formed on a device go to devices with the same px index; at most 2 go from one device to one device, and in every draw exactly 2 for each pair that is used.
All inputs are finite; a program needn't handle non-finite values.
Results may differ from a plain program's by a relative error of at most 0.0049.
Values may be sent and summed in bfloat16 or wider, within the bound.
No kernel may reach another device: no remote copies, remote signals or barrier semaphores. Data moves between devices by JAX's collectives and lax.ppermute only.
A program may use at most 384 MiB of HBM per device.

v0:
```python
import jax
import jax.numpy as jnp
from jax import lax
from jax.experimental import pallas as pl
from jax.experimental.pallas import tpu as pltpu
from jax.sharding import PartitionSpec as P

B = 64
FLAT = B * B
LANES = 128
HALF = B // 2
S = 27
AGG = 6
CCAP = 2
GROUP = 8
TILES = FLAT // LANES
KROWS = GROUP * TILES
MIB = 1 << 20


def lane_low(rows):
    return lax.broadcasted_iota(jnp.int32, (rows, LANES), 1) < B


def swap_halves(x):
    return pltpu.roll(x, B, 1)


def as_tiles(x):
    lead, rows = x.shape[:-2], x.shape[-2]
    split = x.reshape(*lead, rows // GROUP, GROUP, TILES, LANES)
    return jnp.swapaxes(split, -3, -2).reshape(*lead, rows // GROUP, KROWS, LANES)


def from_tiles(x):
    lead, groups = x.shape[:-3], x.shape[-3]
    split = x.reshape(*lead, groups, TILES, GROUP, LANES)
    return jnp.swapaxes(split, -3, -2).reshape(*lead, groups * GROUP, FLAT)


def block_perm(transposed):
    block_axis, tile_axis = (1, 0) if transposed else (0, 1)
    shape = (KROWS, KROWS)
    block_row = lax.broadcasted_iota(jnp.int32, shape, block_axis)
    tile_row = lax.broadcasted_iota(jnp.int32, shape, tile_axis)
    same_r = (block_row // HALF) == (tile_row % GROUP)
    want = 2 * ((tile_row % LANES) // GROUP) + tile_row // LANES
    same_j = (block_row % HALF) == want
    return jnp.where(same_r & same_j, 1.0, 0.0).astype(jnp.bfloat16)


def pack_kernel(send_ref, p_ref, out_ref, own_ref, table_ref):
    groups = p_ref.shape[0]
    rows = groups * GROUP
    slots, peers = send_ref.shape
    perm = block_perm(False)
    low = lane_low(LANES)

    def to_blocks(g):
        top, bottom = p_ref[g, 0:LANES, :], p_ref[g, LANES:KROWS, :]
        even = jnp.where(low, top, swap_halves(bottom))
        odd = jnp.where(low, swap_halves(top), bottom)
        return jnp.concatenate([even, odd], axis=0)

    for g in range(0, groups, 2):
        both = jnp.concatenate([to_blocks(g), to_blocks(g + 1)], axis=1)
        blocks = jnp.dot(perm, both, preferred_element_type=jnp.float32).astype(jnp.bfloat16)
        for h in range(2):
            piece = blocks[:, h * LANES : (h + 1) * LANES].reshape(GROUP, HALF, LANES)
            table_ref[pl.ds((g + h) * GROUP, GROUP)] = piece
    table_ref[rows] = jnp.zeros((HALF, LANES), jnp.bfloat16)
    own_ref[...] = table_ref[0:rows]

    def fill(peer, carry):
        for slot in range(slots):
            wanted = send_ref[slot, peer]
            out_ref[peer * slots + slot] = table_ref[jnp.where(wanted < 0, rows, wanted)]
        return carry

    lax.fori_loop(0, peers, fill, 0)


def project_kernel(a_ref, p_ref, out_ref, left_ref):
    per_row = a_ref.shape[0]
    pairs = out_ref.shape[2]
    flipped = p_ref[0].T
    row_of = lax.broadcasted_iota(jnp.int32, (B, KROWS), 1) % GROUP
    zero = jnp.zeros((B, KROWS), jnp.bfloat16)
    for r in range(GROUP):
        mine = row_of == r
        left_ref[r * B : (r + 1) * B, 0:KROWS] = jnp.where(mine, flipped[0:B], zero)
        left_ref[r * B : (r + 1) * B, KROWS:] = jnp.where(mine, flipped[B:], zero)
    low = lane_low(KROWS)

    def pair_of(pair):
        first = a_ref[2 * pair, 0]
        second = a_ref[min(2 * pair + 1, per_row - 1), 0]
        even = jnp.where(low, first, swap_halves(second))
        odd = jnp.where(low, swap_halves(first), second)
        return jnp.concatenate([even, odd], axis=0)

    for pair in range(0, pairs, 2):
        right = jnp.concatenate([pair_of(pair), pair_of(pair + 1)], axis=1)
        both = jnp.dot(left_ref[...], right, preferred_element_type=jnp.float32).astype(jnp.bfloat16)
        for h in range(2):
            out_ref[0, :, pair + h] = both[:, h * LANES : (h + 1) * LANES].reshape(GROUP, B, LANES)


def combine_kernel(
    source_ref, slot_ref, agg_ref, target_ref, t_ref, own_ref, ghost_ref, out_ref,
    table_ref, even_ref, odd_ref, bucket_ref, place_ref, count_ref,
):
    step = pl.program_id(0)
    per_row, rows = source_ref.shape
    ghosts = ghost_ref.shape[0]
    coarse_here = target_ref.shape[0]
    peers = out_ref.shape[0]
    pairs = t_ref.shape[2]
    low = lane_low(HALF)
    zero_half = jnp.zeros((HALF, LANES), jnp.bfloat16)
    nothing, unused = rows + ghosts, coarse_here * S

    @pl.when(step == 0)
    def _():
        def expand(ref, base):
            def one(i, carry):
                block = ref[i]
                turned = swap_halves(block)
                table_ref[base + i, 0:HALF] = jnp.where(low, block, turned)
                table_ref[base + i, HALF:] = jnp.where(low, turned, block)
                return carry

            lax.fori_loop(0, ref.shape[0], one, 0, unroll=8)

        expand(own_ref, 0)
        expand(ghost_ref, rows)
        table_ref[nothing] = jnp.zeros((B, LANES), jnp.bfloat16)

        def clear(i, carry):
            even_ref[i] = jnp.zeros((HALF, LANES), jnp.float32)
            odd_ref[i] = jnp.zeros((HALF, LANES), jnp.float32)
            return carry

        lax.fori_loop(0, unused, clear, 0, unroll=8)

    low_all = lane_low(B)
    zero_all = jnp.zeros((B, LANES), jnp.bfloat16)

    def one_row(r, carry):
        row = step * GROUP + r
        base = agg_ref[row] * S
        for pair in range(pairs):
            k0, k1 = 2 * pair, 2 * pair + 1
            first = jnp.where(low_all, table_ref[source_ref[k0, row]], zero_all)
            if k1 < per_row:
                second = jnp.where(low_all, zero_all, table_ref[source_ref[k1, row]])
            else:
                second = zero_all
            weights = jnp.concatenate([first, second], axis=0)
            value = jnp.dot(t_ref[0, r, pair], weights, preferred_element_type=jnp.float32)
            top, bottom = value[0:HALF], value[HALF:]
            to0 = base + slot_ref[k0, row]
            even_ref[to0] += jnp.where(low, top, swap_halves(bottom))
            if k1 < per_row:
                to1 = base + slot_ref[k1, row]
                odd_ref[to1] += jnp.where(low, swap_halves(top), bottom)
        return carry

    lax.fori_loop(0, GROUP, one_row, 0)

    @pl.when(step == pl.num_programs(0) - 1)
    def _():
        for p in range(peers):
            count_ref[p] = 0
            for q in range(CCAP):
                place_ref[p * CCAP + q] = -1

        def assign(c, carry):
            target = target_ref[c]
            peer = target // coarse_here % peers
            bucket = peer * CCAP + count_ref[peer]
            count_ref[peer] = count_ref[peer] + 1
            bucket_ref[c] = bucket
            place_ref[bucket] = target % coarse_here
            return carry

        lax.fori_loop(0, coarse_here, assign, 0)
        payload = CCAP * S * HALF
        second_slot = lax.broadcasted_iota(jnp.int32, (out_ref.shape[1] - payload, LANES), 1) // HALF % CCAP

        def note(p, carry):
            value = jnp.full(second_slot.shape, -1, jnp.int32)
            for q in range(CCAP):
                value = jnp.where(second_slot == q, place_ref[p * CCAP + q], value)
            out_ref[p, payload:] = value.astype(jnp.float32).astype(jnp.bfloat16)
            return carry

        lax.fori_loop(0, peers, note, 0)

        def finish(c, carry):
            bucket = bucket_ref[c]
            peer = bucket // CCAP
            start = bucket % CCAP * (S * HALF)
            for s in range(S):
                total = even_ref[c * S + s] + odd_ref[c * S + s]
                here = pl.multiple_of(start + s * HALF, HALF)
                out_ref[peer, pl.ds(here, HALF)] = total.astype(jnp.bfloat16)
            return carry

        lax.fori_loop(0, coarse_here, finish, 0)


def place_kernel(in_ref, out_ref, from_ref):
    step = pl.program_id(0)
    peers = in_ref.shape[0]
    per_step, groups = out_ref.shape[0], out_ref.shape[1]
    payload = CCAP * S * HALF

    @pl.when(step == 0)
    def _():
        for p in range(peers):
            notes = in_ref[p, payload:].astype(jnp.float32)
            which = lax.broadcasted_iota(jnp.int32, notes.shape, 1) // HALF
            for q in range(CCAP):
                place = jnp.max(jnp.where(which == q, notes, -1.0)).astype(jnp.int32)

                @pl.when(place >= 0)
                def _():
                    from_ref[place] = p * CCAP + q

    perm = block_perm(True)
    low = lane_low(LANES)
    for i in range(per_step):
        s = step * per_step + i
        columns = []
        for g in range(groups):
            blocks = []
            for c in range(GROUP):
                bucket = from_ref[g * GROUP + c]
                here = pl.multiple_of((bucket % CCAP * S + s) * HALF, HALF)
                blocks.append(in_ref[bucket // CCAP, pl.ds(here, HALF)])
            columns.append(jnp.concatenate(blocks, axis=0))
        moved = jnp.dot(perm, jnp.concatenate(columns, axis=1), preferred_element_type=jnp.float32)
        moved = moved.astype(jnp.bfloat16)
        for g in range(groups):
            mine = moved[:, g * LANES : (g + 1) * LANES]
            even, odd = mine[0:LANES], mine[LANES:]
            out_ref[i, g, 0:LANES] = jnp.where(low, even, swap_halves(odd))
            out_ref[i, g, LANES:] = jnp.where(low, swap_halves(even), odd)


def whole(shape):
    return pl.BlockSpec(shape, lambda *_: (0,) * len(shape))


def body(a_blocks, p_blocks, a_source, send_list, agg_local, coarse_slot, coarse_target):
    rows, per_row, _ = a_blocks.shape
    peers = lax.axis_size(("px", "py"))
    peers_y = lax.axis_size("py")
    slots = send_list.shape[2]
    coarse_here = rows // AGG
    groups = rows // GROUP
    pairs = (per_row + 3) // 4 * 2
    bf16 = jnp.bfloat16
    smem = pl.BlockSpec(memory_space=pltpu.SMEM)

    a_tiles = as_tiles(a_blocks.transpose(1, 0, 2))
    p_tiles = as_tiles(p_blocks)
    outgoing, own = pl.pallas_call(
        pack_kernel,
        in_specs=[smem, whole((groups, KROWS, LANES))],
        out_specs=[whole((peers * slots, HALF, LANES)), whole((rows, HALF, LANES))],
        out_shape=[
            jax.ShapeDtypeStruct((peers * slots, HALF, LANES), bf16),
            jax.ShapeDtypeStruct((rows, HALF, LANES), bf16),
        ],
        scratch_shapes=[pltpu.VMEM((rows + 1, HALF, LANES), bf16)],
        compiler_params=pltpu.CompilerParams(vmem_limit_bytes=24 * MIB),
    )(send_list[0].T, p_tiles)
    arrived = lax.all_to_all(
        outgoing.reshape(peers, slots, HALF, LANES), ("px", "py"), split_axis=0, concat_axis=0, tiled=True
    ).reshape(peers * slots, HALF, LANES)

    projected = pl.pallas_call(
        project_kernel,
        grid=(groups,),
        in_specs=[
            pl.BlockSpec((per_row, 1, KROWS, LANES), lambda g: (0, g, 0, 0)),
            pl.BlockSpec((1, KROWS, LANES), lambda g: (g, 0, 0)),
        ],
        out_specs=pl.BlockSpec((1, GROUP, pairs, B, LANES), lambda g: (g, 0, 0, 0, 0)),
        out_shape=jax.ShapeDtypeStruct((groups, GROUP, pairs, B, LANES), bf16),
        scratch_shapes=[pltpu.VMEM((GROUP * B, 2 * KROWS), bf16)],
        compiler_params=pltpu.CompilerParams(vmem_limit_bytes=40 * MIB),
        cost_estimate=pl.CostEstimate(
            flops=2 * 512 * 512 * 128 * pairs * groups, bytes_accessed=45_000_000, transcendentals=0
        ),
    )(a_tiles, p_tiles)

    sums = coarse_here * S
    coarse_rows = CCAP * S * HALF + 16
    sent = pl.pallas_call(
        combine_kernel,
        grid=(groups,),
        in_specs=[
            smem, smem, smem, smem,
            pl.BlockSpec((1, GROUP, pairs, B, LANES), lambda g: (g, 0, 0, 0, 0)),
            whole((rows, HALF, LANES)),
            whole((peers * slots, HALF, LANES)),
        ],
        out_specs=whole((peers_y, coarse_rows, LANES)),
        out_shape=jax.ShapeDtypeStruct((peers_y, coarse_rows, LANES), bf16),
        scratch_shapes=[
            pltpu.VMEM((rows + peers * slots + 1, B, LANES), bf16),
            pltpu.VMEM((sums, HALF, LANES), jnp.float32),
            pltpu.VMEM((sums, HALF, LANES), jnp.float32),
            pltpu.SMEM((coarse_here,), jnp.int32),
            pltpu.SMEM((peers_y * CCAP,), jnp.int32),
            pltpu.SMEM((peers_y,), jnp.int32),
        ],
        compiler_params=pltpu.CompilerParams(vmem_limit_bytes=60 * MIB),
    )(a_source.T, coarse_slot.T, agg_local, coarse_target, projected, own, arrived)

    received = lax.all_to_all(sent, "py", split_axis=0, concat_axis=0, tiled=True)

    per_step = 3
    out_groups = coarse_here // GROUP
    placed = pl.pallas_call(
        place_kernel,
        grid=(S // per_step,),
        in_specs=[whole((peers_y, coarse_rows, LANES))],
        out_specs=pl.BlockSpec((per_step, out_groups, KROWS, LANES), lambda s: (s, 0, 0, 0)),
        out_shape=jax.ShapeDtypeStruct((S, out_groups, KROWS, LANES), bf16),
        scratch_shapes=[pltpu.SMEM((coarse_here,), jnp.int32)],
        compiler_params=pltpu.CompilerParams(vmem_limit_bytes=24 * MIB),
    )(received)
    return from_tiles(placed).transpose(1, 0, 2)


def solution(mesh):
    rows = ("px", "py")
    in_specs = (
        P(rows, None, None),
        P(rows, None),
        P(rows, None),
        P(rows, None, None),
        P(rows),
        P(rows, None),
        P(rows),
    )
    return jax.shard_map(body, mesh=mesh, in_specs=in_specs, out_specs=P(rows, None, None), check_vma=False)
```

profile of v0, /device:TPU:0, one launch (start us, length us, event | category | flops | bytes accessed | tf_op | source)
XLA Modules:
  0.0 159.4 jit_solution(1459885087913617103)
XLA Ops:
  0.0 0.0 copy-start
  0.0 1.1 copy-done
  1.1 0.0 copy-start.3
  1.1 0.7 copy-done.3
  1.8 0.0 copy-start.1
  1.8 3.1 %shard_map.74 = (bf16[256,32,128]{2,1,0:T(8,128)(2,1)}, bf16[96,32,128]{2,1,0:T(8,128)(2,1)S(1)}) custom-call(s32[8,32]{1,0:T(8,128)S(1)} %bitcast.28, bf16[12,256,128]{2,1,0:T(8,128)(2,1)S(1)} %bitcast.26), custom_call_target="tpu_custom_call" | custom-call | tf_op jit(solution)/shard_map/pallas_call | solution.py:269
  4.9 0.0 copy-start.2
  4.9 0.9 copy-done.2
  5.9 7.3 %all-to-all-start = ((bf16[32,8,32,128]{3,2,1,0:T(8,128)(2,1)}), bf16[32,8,32,128]{3,2,1,0:T(8,128)(2,1)S(1)}, u32[]{:S(2)}, u32[]{:S(2)}) async-start(bf16[32,8,32,128]{3,2,1,0:T(8,128)(2,1)} %bitcast.13), calls=%async_computation | async-start | bytes 4194304 | tf_op jit(solution)/shard_map/all_to_all | solution.py:280
  13.2 0.0 copy-done.1
  13.2 23.0 %shard_map.73.t_ref = bf16[12,8,14,64,128]{4,3,2,1,0:T(8,128)(2,1)} custom-call(bf16[27,12,256,128]{3,2,1,0:T(8,128)(2,1)} %bitcast.29, bf16[12,256,128]{2,1,0:T(8,128)(2,1)S(1)} %bitcast.27), custom_call_target="tpu_custom_call" | custom-call | flops 11274289152 | bytes 45000000 | tf_op jit(solution)/shard_map/pallas_call | solution.py:284
  36.2 25.9 %all-to-all-done = bf16[32,8,32,128]{3,2,1,0:T(8,128)(2,1)S(1)} async-done(((bf16[32,8,32,128]{3,2,1,0:T(8,128)(2,1)}), bf16[32,8,32,128]{3,2,1,0:T(8,128)(2,1)S(1)}, u32[]{:S(2)}, u32[]{:S(2)}) %all-to-all-start) | async-done | bytes 2097184 | tf_op jit(solution)/shard_map/all_to_all | solution.py:280
  62.1 0.0 copy-start.4
  62.1 1.3 copy-done.4
  63.4 43.3 %shard_map.75 = bf16[8,1744,128]{2,1,0:T(8,128)(2,1)} custom-call(s32[27,96]{1,0:T(8,128)} %bitcast.31, s32[27,96]{1,0:T(8,128)} %bitcast.32, s32[96]{0:T(128)} %agg_ref.1, s32[16]{0:T(128)} %target_ref.1, bf16[12,8,14,64,128]{4,3,2,1,0:T(8,128)(2,1)} %shard_map.73.t_ref, bf16[96,32,128]{2,1,0:T(8,128)(2,1)} %copy-done.2, bf16[256,32,128]{2,1,0:T(8,128)(2,1)} %bitcast.30), custom_call_target="tpu_custom_call" | custom-call | tf_op jit(solution)/shard_map/pallas_call | solution.py:302
  106.7 46.0 %all_to_all.10.in_ref = bf16[8,1744,128]{2,1,0:T(8,128)(2,1)S(1)} all-to-all(bf16[8,1744,128]{2,1,0:T(8,128)(2,1)} %shard_map.75), channel_id=1, replica_groups=mesh['px'=4,'py'=8] {'py'}, dimensions={0} | all-to-all | bytes 7143424 | tf_op jit(solution)/shard_map/all_to_all | solution.py:324
  152.6 6.8 %shard_map.76 = bf16[27,2,256,128]{3,2,1,0:T(8,128)(2,1)} custom-call(bf16[8,1744,128]{2,1,0:T(8,128)(2,1)S(1)} %all_to_all.10.in_ref), custom_call_target="tpu_custom_call" | custom-call | tf_op jit(solution)/shard_map/pallas_call | solution.py:328
Async XLA Ops:
  0.0 1.1 copy-start
  1.1 0.7 copy-start.3
  1.8 11.4 %copy-start.1 = (bf16[96,4096]{1,0:T(8,128)(2,1)S(1)}, bf16[96,4096]{1,0:T(8,128)(2,1)}, u32[]{:S(2)}) copy-start(bf16[96,4096]{1,0:T(8,128)(2,1)} %param.8) | copy-start | bytes 2359300
  4.9 0.9 copy-start.2
  5.9 56.2 %all-to-all-start = ((bf16[32,8,32,128]{3,2,1,0:T(8,128)(2,1)}), bf16[32,8,32,128]{3,2,1,0:T(8,128)(2,1)S(1)}, u32[]{:S(2)}, u32[]{:S(2)}) async-start(bf16[32,8,32,128]{3,2,1,0:T(8,128)(2,1)} %bitcast.13), calls=%async_computation | async-start | bytes 4194304 | tf_op jit(solution)/shard_map/all_to_all | solution.py:280
  62.1 1.3 copy-start.4
where the time goes:
time: 160 us; the launch traced here: 159 us
  Pallas kernels  76.1 us (48%)
  blocking collectives  46 us (29%)
  waiting for transfers between devices  25.9 us (16%)
  starting transfers between devices  7.3 us (5%)
  local copies, waits for them, and re-layouts  4.08 us (3%)
    all_to_all x1, blocking collectives, body(): lax.all_to_all(sent, 'py', split_axis=0, concat_axis=0, tiled=True)  46 us
    pallas_call x1, Pallas kernels, body(): pl.pallas_call(combine_kernel, grid=(groups,), in_specs=[smem, smem, smem...  43.3 us
    all_to_all x1, waiting for transfers between devices, body(): lax.all_to_all(outgoing.reshape(peers, slots, HALF, LANES), ('px', 'py'),...  25.9 us
    pallas_call x1, Pallas kernels, body(): pl.pallas_call(project_kernel, grid=(groups,), in_specs=[pl.BlockSpec((pe...  23 us
    all_to_all x1, starting transfers between devices, body(): lax.all_to_all(outgoing.reshape(peers, slots, HALF, LANES), ('px', 'py'),...  7.3 us
    pallas_call x1, Pallas kernels, body(): pl.pallas_call(place_kernel, grid=(S // per_step,), in_specs=[whole((peer...  6.79 us
    unnamed x10, local copies, waits for them, and re-layouts  4.08 us
  transfers between devices with their start and end apart: 1, of which 1 were waited for; matrix products, arithmetic and copies ran while one was open for 0% of the time, Pallas kernels for 14%

commit v1 on v0

--- a/solution.py
+++ b/solution.py
@@ -1,3 +1,5 @@
+import functools
+
 import jax
 import jax.numpy as jnp
 from jax import lax
@@ -15,6 +17,8 @@
 GROUP = 8
 TILES = FLAT // LANES
 KROWS = GROUP * TILES
+CHUNK = 16
+RING = 4
 MIB = 1 << 20
 
 
@@ -80,9 +84,47 @@
     lax.fori_loop(0, peers, fill, 0)
 
 
-def project_kernel(a_ref, p_ref, out_ref, left_ref):
-    per_row = a_ref.shape[0]
-    pairs = out_ref.shape[2]
+def fold(value, low):
+    top, bottom = value[0:HALF], value[HALF:]
+    return jnp.where(low, top, swap_halves(bottom)), jnp.where(low, swap_halves(top), bottom)
+
+
+def project_kernel(
+    ghosts, source_ref, slot_ref, agg_ref, a_ref, p_ref, own_ref, sum_ref, tiles_hbm, meta_ref, count_ref,
+    left_ref, first_ref, second_ref, odd_ref, even_tiles, odd_tiles, merged_ref, done_ref, sems,
+):
+    step = pl.program_id(0)
+    per_row, rows = source_ref.shape
+    pairs = (per_row + 3) // 4 * 2
+    unused = sum_ref.shape[0]
+    low_half, low_all = lane_low(HALF), lane_low(B)
+    zero_all = jnp.zeros((B, LANES), jnp.bfloat16)
+
+    @pl.when(step == 0)
+    def _():
+        done_ref[0] = 0
+
+        def expand(i, carry):
+            block = own_ref[i]
+            turned = swap_halves(block)
+            zero = jnp.zeros((HALF, LANES), jnp.bfloat16)
+            first_ref[i, 0:HALF] = jnp.where(low_half, block, zero)
+            first_ref[i, HALF:] = jnp.where(low_half, turned, zero)
+            second_ref[i, 0:HALF] = jnp.where(low_half, zero, turned)
+            second_ref[i, HALF:] = jnp.where(low_half, zero, block)
+            return carry
+
+        lax.fori_loop(0, rows, expand, 0, unroll=8)
+        first_ref[rows] = zero_all
+        second_ref[rows] = zero_all
+
+        def clear(i, carry):
+            sum_ref[i] = jnp.zeros((HALF, LANES), jnp.float32)
+            odd_ref[i] = jnp.zeros((HALF, LANES), jnp.float32)
+            return carry
+
+        lax.fori_loop(0, unused, clear, 0, unroll=8)
+
     flipped = p_ref[0].T
     row_of = lax.broadcasted_iota(jnp.int32, (B, KROWS), 1) % GROUP
     zero = jnp.zeros((B, KROWS), jnp.bfloat16)
@@ -99,115 +141,205 @@
         odd = jnp.where(low, swap_halves(first), second)
         return jnp.concatenate([even, odd], axis=0)
 
+    before = done_ref[0]
+    even_count = jnp.int32(0)
+    odd_count = jnp.int32(0)
     for pair in range(0, pairs, 2):
         right = jnp.concatenate([pair_of(pair), pair_of(pair + 1)], axis=1)
         both = jnp.dot(left_ref[...], right, preferred_element_type=jnp.float32).astype(jnp.bfloat16)
-        for h in range(2):
-            out_ref[0, :, pair + h] = both[:, h * LANES : (h + 1) * LANES].reshape(GROUP, B, LANES)
+        for r in range(GROUP):
+            row = step * GROUP + r
+            base = agg_ref[row] * S
+            moving = both[r * B : (r + 1) * B]
+            weights, targets = [], []
+            for h in range(2):
+                tile = moving[:, h * LANES : (h + 1) * LANES]
+                k0, k1 = 2 * (pair + h), 2 * (pair + h) + 1
+                source = source_ref[k0, row]
+                target = base + slot_ref[k0, row]
+                upper = first_ref[jnp.minimum(source, rows)]
+                targets.append(target)
+                if k0 > 0:
+                    even_tiles[even_count] = tile
+                    meta_ref[0, before + even_count] = jnp.maximum(source - rows, 0) * 1024 + target
+                    even_count += (source >= rows).astype(jnp.int32)
+                if k1 < per_row:
+                    source = source_ref[k1, row]
+                    target = base + slot_ref[k1, row]
+                    lower = second_ref[jnp.minimum(source, rows)]
+                    targets.append(target)
+                    odd_tiles[odd_count] = tile
+                    meta_ref[1, before + odd_count] = jnp.maximum(source - rows, 0) * 1024 + target
+                    odd_count += (source >= rows).astype(jnp.int32)
+                else:
+                    lower = zero_all
+                    targets.append(None)
+                filled = jnp.concatenate([upper, lower], axis=0)
+                blank = jnp.zeros_like(filled)
+                weights.append(jnp.concatenate([filled, blank] if h == 0 else [blank, filled], axis=1))
+            value = jnp.dot(moving, jnp.concatenate(weights, axis=0), preferred_element_type=jnp.float32)
+            for h in range(2):
+                even, odd = fold(value[:, h * LANES : (h + 1) * LANES], low_half)
+                sum_ref[targets[2 * h]] += even
+                if targets[2 * h + 1] is not None:
+                    odd_ref[targets[2 * h + 1]] += odd
+
+    after = jnp.maximum(even_count, odd_count)
+    no_entry = ghosts * 1024 + unused
+
+    def merge(i, carry):
+        keep_even = jnp.where(low_all, i, after) < even_count
+        keep_odd = jnp.where(low_all, after, i) < odd_count
+        tile = jnp.where(keep_even, even_tiles[i], zero_all)
+        merged_ref[before + i] = jnp.where(keep_odd, odd_tiles[i], tile)
+        meta_ref[0, before + i] = jnp.where(i < even_count, meta_ref[0, before + i], no_entry)
+        meta_ref[1, before + i] = jnp.where(i < odd_count, meta_ref[1, before + i], no_entry)
+        return carry
+
+    lax.fori_loop(0, after, merge, 0)
+    done_ref[0] = before + after
+
+    @pl.when(step == pl.num_programs(0) - 1)
+    def _():
+        def total(i, carry):
+            sum_ref[i] += odd_ref[i]
+            return carry
+
+        lax.fori_loop(0, unused, total, 0, unroll=8)
+        found = before + after
+        chunks = (found + CHUNK - 1) // CHUNK
+
+        def pad(i, carry):
+            merged_ref[i] = zero_all
+            meta_ref[0, i] = no_entry
+            meta_ref[1, i] = no_entry
+            return carry
+
+        lax.fori_loop(found, chunks * CHUNK, pad, 0)
+        count_ref[0] = chunks
+
+        def copy(i):
+            span = pl.ds(i * CHUNK, CHUNK)
+            return pltpu.make_async_copy(merged_ref.at[span], tiles_hbm.at[span], sems.at[i % RING])
+
+        def send(i, carry):
+            @pl.when(i >= RING)
+            def _():
+                copy(i - RING).wait()
+
+            copy(i).start()
+            return carry
+
+        lax.fori_loop(0, chunks, send, 0)
+        lax.fori_loop(jnp.maximum(chunks - RING, 0), chunks, lambda i, c: (copy(i).wait(), c)[1], 0)
 
 
 def combine_kernel(
-    source_ref, slot_ref, agg_ref, target_ref, t_ref, own_ref, ghost_ref, out_ref,
-    table_ref, even_ref, odd_ref, bucket_ref, place_ref, count_ref,
+    meta_ref, count_ref, target_ref, ghost_ref, sum_hbm, tiles_hbm, out_ref,
+    table_ref, even_ref, odd_ref, tiles_ref, bucket_ref, place_ref, per_peer_ref, sum_sem, sems,
 ):
-    step = pl.program_id(0)
-    per_row, rows = source_ref.shape
     ghosts = ghost_ref.shape[0]
     coarse_here = target_ref.shape[0]
+    unused = coarse_here * S
     peers = out_ref.shape[0]
-    pairs = t_ref.shape[2]
-    low = lane_low(HALF)
-    zero_half = jnp.zeros((HALF, LANES), jnp.bfloat16)
-    nothing, unused = rows + ghosts, coarse_here * S
-
-    @pl.when(step == 0)
-    def _():
-        def expand(ref, base):
-            def one(i, carry):
-                block = ref[i]
-                turned = swap_halves(block)
-                table_ref[base + i, 0:HALF] = jnp.where(low, block, turned)
-                table_ref[base + i, HALF:] = jnp.where(low, turned, block)
-                return carry
-
-            lax.fori_loop(0, ref.shape[0], one, 0, unroll=8)
-
-        expand(own_ref, 0)
-        expand(ghost_ref, rows)
-        table_ref[nothing] = jnp.zeros((B, LANES), jnp.bfloat16)
-
-        def clear(i, carry):
-            even_ref[i] = jnp.zeros((HALF, LANES), jnp.float32)
-            odd_ref[i] = jnp.zeros((HALF, LANES), jnp.float32)
-            return carry
-
-        lax.fori_loop(0, unused, clear, 0, unroll=8)
-
-    low_all = lane_low(B)
+    chunks = count_ref[0]
+    low_half, low_all = lane_low(HALF), lane_low(B)
     zero_all = jnp.zeros((B, LANES), jnp.bfloat16)
-
-    def one_row(r, carry):
-        row = step * GROUP + r
-        base = agg_ref[row] * S
-        for pair in range(pairs):
-            k0, k1 = 2 * pair, 2 * pair + 1
-            first = jnp.where(low_all, table_ref[source_ref[k0, row]], zero_all)
-            if k1 < per_row:
-                second = jnp.where(low_all, zero_all, table_ref[source_ref[k1, row]])
-            else:
-                second = zero_all
-            weights = jnp.concatenate([first, second], axis=0)
-            value = jnp.dot(t_ref[0, r, pair], weights, preferred_element_type=jnp.float32)
-            top, bottom = value[0:HALF], value[HALF:]
-            to0 = base + slot_ref[k0, row]
-            even_ref[to0] += jnp.where(low, top, swap_halves(bottom))
-            if k1 < per_row:
-                to1 = base + slot_ref[k1, row]
-                odd_ref[to1] += jnp.where(low, swap_halves(top), bottom)
-        return carry
-
-    lax.fori_loop(0, GROUP, one_row, 0)
-
-    @pl.when(step == pl.num_programs(0) - 1)
-    def _():
-        for p in range(peers):
-            count_ref[p] = 0
-            for q in range(CCAP):
-                place_ref[p * CCAP + q] = -1
-
-        def assign(c, carry):
-            target = target_ref[c]
-            peer = target // coarse_here % peers
-            bucket = peer * CCAP + count_ref[peer]
-            count_ref[peer] = count_ref[peer] + 1
-            bucket_ref[c] = bucket
-            place_ref[bucket] = target % coarse_here
-            return carry
-
-        lax.fori_loop(0, coarse_here, assign, 0)
-        payload = CCAP * S * HALF
-        second_slot = lax.broadcasted_iota(jnp.int32, (out_ref.shape[1] - payload, LANES), 1) // HALF % CCAP
-
-        def note(p, carry):
-            value = jnp.full(second_slot.shape, -1, jnp.int32)
-            for q in range(CCAP):
-                value = jnp.where(second_slot == q, place_ref[p * CCAP + q], value)
-            out_ref[p, payload:] = value.astype(jnp.float32).astype(jnp.bfloat16)
-            return carry
-
-        lax.fori_loop(0, peers, note, 0)
-
-        def finish(c, carry):
-            bucket = bucket_ref[c]
-            peer = bucket // CCAP
-            start = bucket % CCAP * (S * HALF)
-            for s in range(S):
-                total = even_ref[c * S + s] + odd_ref[c * S + s]
-                here = pl.multiple_of(start + s * HALF, HALF)
-                out_ref[peer, pl.ds(here, HALF)] = total.astype(jnp.bfloat16)
-            return carry
-
-        lax.fori_loop(0, coarse_here, finish, 0)
+    load_sums = pltpu.make_async_copy(sum_hbm, even_ref.at[pl.ds(0, unused)], sum_sem)
+    load_sums.start()
+
+    def fetch(i):
+        slot = i % RING
+        return pltpu.make_async_copy(tiles_hbm.at[pl.ds(i * CHUNK, CHUNK)], tiles_ref.at[slot], sems.at[slot])
+
+    for i in range(RING - 1):
+
+        @pl.when(i < chunks)
+        def _():
+            fetch(i).start()
+
+    def expand(i, carry):
+        block = ghost_ref[i]
+        turned = swap_halves(block)
+        table_ref[i, 0:HALF] = jnp.where(low_half, block, turned)
+        table_ref[i, HALF:] = jnp.where(low_half, turned, block)
+        return carry
+
+    lax.fori_loop(0, ghosts, expand, 0, unroll=8)
+    table_ref[ghosts] = zero_all
+
+    def clear(i, carry):
+        odd_ref[i] = jnp.zeros((HALF, LANES), jnp.float32)
+        return carry
+
+    lax.fori_loop(0, unused, clear, 0, unroll=8)
+
+    for p in range(peers):
+        per_peer_ref[p] = 0
+        for q in range(CCAP):
+            place_ref[p * CCAP + q] = -1
+
+    def assign(c, carry):
+        target = target_ref[c]
+        peer = target // coarse_here % peers
+        bucket = peer * CCAP + per_peer_ref[peer]
+        per_peer_ref[peer] = per_peer_ref[peer] + 1
+        bucket_ref[c] = bucket
+        place_ref[bucket] = target % coarse_here
+        return carry
+
+    lax.fori_loop(0, coarse_here, assign, 0)
+    payload = CCAP * S * HALF
+    second_slot = lax.broadcasted_iota(jnp.int32, (out_ref.shape[1] - payload, LANES), 1) // HALF % CCAP
+
+    def note(p, carry):
+        value = jnp.full(second_slot.shape, -1, jnp.int32)
+        for q in range(CCAP):
+            value = jnp.where(second_slot == q, place_ref[p * CCAP + q], value)
+        out_ref[p, payload:] = value.astype(jnp.float32).astype(jnp.bfloat16)
+        return carry
+
+    lax.fori_loop(0, peers, note, 0)
+    load_sums.wait()
+
+    def work(i, carry):
+        @pl.when(i + RING - 1 < chunks)
+        def _():
+            fetch(i + RING - 1).start()
+
+        fetch(i).wait()
+        slot = i % RING
+        for j in range(0, CHUNK, 2):
+            weights, targets = [], []
+            for h in range(2):
+                at = i * CHUNK + j + h
+                even, odd = meta_ref[0, at], meta_ref[1, at]
+                upper = jnp.where(low_all, table_ref[even // 1024], zero_all)
+                lower = jnp.where(low_all, zero_all, table_ref[odd // 1024])
+                targets += [even % 1024, odd % 1024]
+                filled = jnp.concatenate([upper, lower], axis=0)
+                blank = jnp.zeros_like(filled)
+                weights.append(jnp.concatenate([filled, blank] if h == 0 else [blank, filled], axis=1))
+            moving = jnp.concatenate([tiles_ref[slot, j], tiles_ref[slot, j + 1]], axis=1)
+            value = jnp.dot(moving, jnp.concatenate(weights, axis=0), preferred_element_type=jnp.float32)
+            for h in range(2):
+                even, odd = fold(value[:, h * LANES : (h + 1) * LANES], low_half)
+                even_ref[targets[2 * h]] += even
+                odd_ref[targets[2 * h + 1]] += odd
+        return carry
+
+    lax.fori_loop(0, chunks, work, 0)
+
+    def finish(c, carry):
+        bucket = bucket_ref[c]
+        start = bucket % CCAP * (S * HALF)
+        for s in range(S):
+            total = even_ref[c * S + s] + odd_ref[c * S + s]
+            here = pl.multiple_of(start + s * HALF, HALF)
+            out_ref[bucket // CCAP, pl.ds(here, HALF)] = total.astype(jnp.bfloat16)
+        return carry
+
+    lax.fori_loop(0, coarse_here, finish, 0)
 
 
 def place_kernel(in_ref, out_ref, from_ref):
@@ -281,45 +413,65 @@
         outgoing.reshape(peers, slots, HALF, LANES), ("px", "py"), split_axis=0, concat_axis=0, tiled=True
     ).reshape(peers * slots, HALF, LANES)
 
-    projected = pl.pallas_call(
-        project_kernel,
+    sums = coarse_here * S
+    most_tiles = (rows * pairs + CHUNK - 1) // CHUNK * CHUNK
+    local, tiles, meta, count = pl.pallas_call(
+        functools.partial(project_kernel, peers * slots),
         grid=(groups,),
         in_specs=[
+            smem, smem, smem,
             pl.BlockSpec((per_row, 1, KROWS, LANES), lambda g: (0, g, 0, 0)),
             pl.BlockSpec((1, KROWS, LANES), lambda g: (g, 0, 0)),
+            whole((rows, HALF, LANES)),
         ],
-        out_specs=pl.BlockSpec((1, GROUP, pairs, B, LANES), lambda g: (g, 0, 0, 0, 0)),
-        out_shape=jax.ShapeDtypeStruct((groups, GROUP, pairs, B, LANES), bf16),
-        scratch_shapes=[pltpu.VMEM((GROUP * B, 2 * KROWS), bf16)],
-        compiler_params=pltpu.CompilerParams(vmem_limit_bytes=40 * MIB),
+        out_specs=[whole((sums, HALF, LANES)), pl.BlockSpec(memory_space=pl.ANY), smem, smem],
+        out_shape=[
+            jax.ShapeDtypeStruct((sums, HALF, LANES), jnp.float32),
+            jax.ShapeDtypeStruct((most_tiles, B, LANES), bf16),
+            jax.ShapeDtypeStruct((2, most_tiles + CHUNK), jnp.int32),
+            jax.ShapeDtypeStruct((1,), jnp.int32),
+        ],
+        scratch_shapes=[
+            pltpu.VMEM((GROUP * B, 2 * KROWS), bf16),
+            pltpu.VMEM((rows + 1, B, LANES), bf16),
+            pltpu.VMEM((rows + 1, B, LANES), bf16),
+            pltpu.VMEM((sums, HALF, LANES), jnp.float32),
+            pltpu.VMEM((GROUP * pairs + 1, B, LANES), bf16),
+            pltpu.VMEM((GROUP * pairs + 1, B, LANES), bf16),
+            pltpu.VMEM((most_tiles, B, LANES), bf16),
+            pltpu.SMEM((1,), jnp.int32),
+            pltpu.SemaphoreType.DMA((RING,)),
+        ],
+        compiler_params=pltpu.CompilerParams(vmem_limit_bytes=60 * MIB),
         cost_estimate=pl.CostEstimate(
-            flops=2 * 512 * 512 * 128 * pairs * groups, bytes_accessed=45_000_000, transcendentals=0
+            flops=4 * 512 * 512 * 128 * pairs * groups, bytes_accessed=45_000_000, transcendentals=0
         ),
-    )(a_tiles, p_tiles)
-
-    sums = coarse_here * S
+    )(a_source.T, coarse_slot.T, agg_local, a_tiles, p_tiles, own)
+
     coarse_rows = CCAP * S * HALF + 16
     sent = pl.pallas_call(
         combine_kernel,
-        grid=(groups,),
         in_specs=[
-            smem, smem, smem, smem,
-            pl.BlockSpec((1, GROUP, pairs, B, LANES), lambda g: (g, 0, 0, 0, 0)),
-            whole((rows, HALF, LANES)),
+            smem, smem, smem,
             whole((peers * slots, HALF, LANES)),
+            pl.BlockSpec(memory_space=pl.ANY),
+            pl.BlockSpec(memory_space=pl.ANY),
         ],
         out_specs=whole((peers_y, coarse_rows, LANES)),
         out_shape=jax.ShapeDtypeStruct((peers_y, coarse_rows, LANES), bf16),
         scratch_shapes=[
-            pltpu.VMEM((rows + peers * slots + 1, B, LANES), bf16),
-            pltpu.VMEM((sums, HALF, LANES), jnp.float32),
-            pltpu.VMEM((sums, HALF, LANES), jnp.float32),
+            pltpu.VMEM((peers * slots + 1, B, LANES), bf16),
+            pltpu.VMEM((sums + 1, HALF, LANES), jnp.float32),
+            pltpu.VMEM((sums + 1, HALF, LANES), jnp.float32),
+            pltpu.VMEM((RING, CHUNK, B, LANES), bf16),
             pltpu.SMEM((coarse_here,), jnp.int32),
             pltpu.SMEM((peers_y * CCAP,), jnp.int32),
             pltpu.SMEM((peers_y,), jnp.int32),
+            pltpu.SemaphoreType.DMA,
+            pltpu.SemaphoreType.DMA((RING,)),
         ],
-        compiler_params=pltpu.CompilerParams(vmem_limit_bytes=60 * MIB),
-    )(a_source.T, coarse_slot.T, agg_local, coarse_target, projected, own, arrived)
+        compiler_params=pltpu.CompilerParams(vmem_limit_bytes=56 * MIB),
+    )(meta, count, coarse_target, arrived, local, tiles)
 
     received = lax.all_to_all(sent, "py", split_axis=0, concat_axis=0, tiled=True)
 

time: 160 us -> 143 us (0.89)
  waiting for transfers between devices: 25.9 us -> 0.01 us
  Pallas kernels: 76.1 us -> 84.4 us
    all_to_all x1, waiting for transfers between devices: 25.9 us -> 0.01 us  [body(): lax.all_to_all(outgoing.reshape(peers, slots, HALF, LANES), ('px', 'py'),...]
    pallas_call x2, Pallas kernels: 66.3 us -> 74.5 us  [the longest x1 53 us: body(): pl.pallas_call(functools.partial(project_kernel, peers * slots), grid=(gr...]
    unnamed x10 -> x8, local copies, waits for them, and re-layouts: 4.08 us -> 4.05 us
  transfers between devices with their start and end apart: 1 -> 1, of which waited for: 1 -> 0; matrix products, arithmetic and copies ran while one was open for 0% -> 0% of each run, Pallas kernels for 14% -> 37%
where the time goes in v1:
time: 143 us; the launch traced here: 142 us
  Pallas kernels  84.4 us (59%)
  blocking collectives  46.4 us (32%)
  starting transfers between devices  7.3 us (5%)
  local copies, waits for them, and re-layouts  4.05 us (3%)
    pallas_call x1, Pallas kernels, body(): pl.pallas_call(functools.partial(project_kernel, peers * slots), grid=(gr...  53 us
    all_to_all x1, blocking collectives, body(): lax.all_to_all(sent, 'py', split_axis=0, concat_axis=0, tiled=True)  46.4 us
    pallas_call x1, Pallas kernels, body(): pl.pallas_call(combine_kernel, in_specs=[smem, smem, smem, whole((peers *...  21.5 us
    all_to_all x1, starting transfers between devices, body(): lax.all_to_all(outgoing.reshape(peers, slots, HALF, LANES), ('px', 'py'),...  7.3 us
    pallas_call x1, Pallas kernels, body(): pl.pallas_call(place_kernel, grid=(S // per_step,), in_specs=[whole((peer...  6.78 us
    unnamed x8, local copies, waits for them, and re-layouts  4.05 us
    pallas_call x1, Pallas kernels, body(): pl.pallas_call(pack_kernel, in_specs=[smem, whole((groups, KROWS, LANES))...  3.1 us
  transfers between devices with their start and end apart: 1, of which 0 were waited for; matrix products, arithmetic and copies ran while one was open for 0% of the time, Pallas kernels for 37%

profile of v1, /device:TPU:0, one launch (start us, length us, event | category | flops | bytes accessed | tf_op | source)
XLA Modules:
  0.0 142.2 jit_solution(15359925820737953848)
XLA Ops:
  0.0 0.0 copy-start
  0.0 1.1 copy-done
  1.1 0.0 copy-start.1
  1.1 0.7 copy-done.1
  1.8 3.1 %shard_map.73 = (bf16[256,32,128]{2,1,0:T(8,128)(2,1)}, bf16[96,32,128]{2,1,0:T(8,128)(2,1)S(1)}) custom-call(s32[8,32]{1,0:T(8,128)S(1)} %bitcast.28, bf16[12,256,128]{2,1,0:T(8,128)(2,1)S(1)} %bitcast.27), custom_call_target="tpu_custom_call" | custom-call | tf_op jit(solution)/shard_map/pallas_call | solution.py:401
  4.9 0.0 copy-start.2
  4.9 0.9 copy-done.2
  5.8 7.3 %all-to-all-start = ((bf16[32,8,32,128]{3,2,1,0:T(8,128)(2,1)}), bf16[32,8,32,128]{3,2,1,0:T(8,128)(2,1)S(1)}, u32[]{:S(2)}, u32[]{:S(2)}) async-start(bf16[32,8,32,128]{3,2,1,0:T(8,128)(2,1)} %bitcast.13), calls=%async_computation | async-start | bytes 4194304 | tf_op jit(solution)/shard_map/all_to_all | solution.py:412
  13.2 53.0 %shard_map.74 = (f32[432,32,128]{2,1,0:T(8,128)}, bf16[1344,64,128]{2,1,0:T(8,128)(2,1)}, s32[2,1360]{1,0:T(2,128)}, s32[1]{0:T(128)}) custom-call(s32[27,96]{1,0:T(8,128)} %bitcast.31, s32[27,96]{1,0:T(8,128)} %bitcast.32, s32[96]{0:T(128)} %agg_ref.1, bf16[27,12,256,128]{3,2,1,0:T(8,128)(2,1)} %bitcast.30, bf16[12,256,128]{2,1,0:T(8,128)(2,1)} %bitcast.26, ...), custom_call_target="tpu_custom_call" | custom-call | flops 22548578304 | bytes 45000000 | tf_op jit(solution)/shard_map/pallas_call | solution.py:418
  66.2 0.0 all-to-all-done
  66.2 0.0 copy-start.3
  66.2 1.3 copy-done.3
  67.5 21.5 %shard_map.75 = bf16[8,1744,128]{2,1,0:T(8,128)(2,1)} custom-call(s32[2,1360]{1,0:T(2,128)} %get-tuple-element.12.meta_ref, s32[1]{0:T(128)} %get-tuple-element.13.count_ref, s32[16]{0:T(128)} %target_ref.1, bf16[256,32,128]{2,1,0:T(8,128)(2,1)} %bitcast.29, f32[432,32,128]{2,1,0:T(8,128)} %get-tuple-element.15.sum_hbm, ...), custom_call_target="tpu_custom_call" | custom-call | tf_op jit(solution)/shard_map/pallas_call | solution.py:452
  89.0 46.4 %all_to_all.10.in_ref = bf16[8,1744,128]{2,1,0:T(8,128)(2,1)S(1)} all-to-all(bf16[8,1744,128]{2,1,0:T(8,128)(2,1)} %shard_map.75), channel_id=1, replica_groups=mesh['px'=4,'py'=8] {'py'}, dimensions={0} | all-to-all | bytes 7143424 | tf_op jit(solution)/shard_map/all_to_all | solution.py:476
  135.4 6.8 %shard_map.76 = bf16[27,2,256,128]{3,2,1,0:T(8,128)(2,1)} custom-call(bf16[8,1744,128]{2,1,0:T(8,128)(2,1)S(1)} %all_to_all.10.in_ref), custom_call_target="tpu_custom_call" | custom-call | tf_op jit(solution)/shard_map/pallas_call | solution.py:480
Async XLA Ops:
  0.0 1.1 copy-start
  1.1 0.7 copy-start.1
  4.9 0.9 copy-start.2
  5.8 60.3 %all-to-all-start = ((bf16[32,8,32,128]{3,2,1,0:T(8,128)(2,1)}), bf16[32,8,32,128]{3,2,1,0:T(8,128)(2,1)S(1)}, u32[]{:S(2)}, u32[]{:S(2)}) async-start(bf16[32,8,32,128]{3,2,1,0:T(8,128)(2,1)} %bitcast.13), calls=%async_computation | async-start | bytes 4194304 | tf_op jit(solution)/shard_map/all_to_all | solution.py:412
  66.2 1.3 copy-start.3

commit v2 on v1

v2 whole, which is shorter than its diff:
```python
import functools

import jax
import jax.numpy as jnp
from jax import lax
from jax.experimental import pallas as pl
from jax.experimental.pallas import tpu as pltpu
from jax.sharding import PartitionSpec as P

B = 64
FLAT = B * B
LANES = 128
HALF = B // 2
S = 27
AGG = 6
CCAP = 2
GROUP = 8
TILES = FLAT // LANES
KROWS = GROUP * TILES
PIECES = 3
PS = S // PIECES
CHUNK = 16
LIST = 128
STAGE = LIST + 2 * CHUNK
SPREAD = 1024
RING = 4
MIB = 1 << 20


def lane_low(rows):
    return lax.broadcasted_iota(jnp.int32, (rows, LANES), 1) < B


def swap_halves(x):
    return pltpu.roll(x, B, 1)


def as_tiles(x):
    lead, rows = x.shape[:-2], x.shape[-2]
    split = x.reshape(*lead, rows // GROUP, GROUP, TILES, LANES)
    return jnp.swapaxes(split, -3, -2).reshape(*lead, rows // GROUP, KROWS, LANES)


def from_tiles(x):
    lead, groups = x.shape[:-3], x.shape[-3]
    split = x.reshape(*lead, groups, TILES, GROUP, LANES)
    return jnp.swapaxes(split, -3, -2).reshape(*lead, groups * GROUP, FLAT)


def block_perm(transposed):
    block_axis, tile_axis = (1, 0) if transposed else (0, 1)
    shape = (KROWS, KROWS)
    block_row = lax.broadcasted_iota(jnp.int32, shape, block_axis)
    tile_row = lax.broadcasted_iota(jnp.int32, shape, tile_axis)
    same_r = (block_row // HALF) == (tile_row % GROUP)
    want = 2 * ((tile_row % LANES) // GROUP) + tile_row // LANES
    same_j = (block_row % HALF) == want
    return jnp.where(same_r & same_j, 1.0, 0.0).astype(jnp.bfloat16)


def pack_kernel(send_hbm, p_hbm, out_ref, own_hbm, send_ref, p_ref, table_ref, sems, send_sem, own_sem):
    groups = p_ref.shape[0]
    rows = groups * GROUP
    slots, peers = send_ref.shape
    get_send = pltpu.make_async_copy(send_hbm, send_ref, send_sem)
    get_send.start()

    def get(g):
        return pltpu.make_async_copy(p_hbm.at[pl.ds(g, 2)], p_ref.at[pl.ds(g, 2)], sems.at[g // 2])

    for g in range(0, groups, 2):
        get(g).start()
    perm = block_perm(False)
    low = lane_low(LANES)

    def to_blocks(g):
        top, bottom = p_ref[g, 0:LANES, :], p_ref[g, LANES:KROWS, :]
        even = jnp.where(low, top, swap_halves(bottom))
        odd = jnp.where(low, swap_halves(top), bottom)
        return jnp.concatenate([even, odd], axis=0)

    for g in range(0, groups, 2):
        get(g).wait()
        both = jnp.concatenate([to_blocks(g), to_blocks(g + 1)], axis=1)
        blocks = jnp.dot(perm, both, preferred_element_type=jnp.float32).astype(jnp.bfloat16)
        for h in range(2):
            piece = blocks[:, h * LANES : (h + 1) * LANES].reshape(GROUP, HALF, LANES)
            table_ref[pl.ds((g + h) * GROUP, GROUP)] = piece
    put_own = pltpu.make_async_copy(table_ref.at[pl.ds(0, rows)], own_hbm, own_sem)
    put_own.start()
    table_ref[rows] = jnp.zeros((HALF, LANES), jnp.bfloat16)
    get_send.wait()

    def fill(peer, carry):
        for slot in range(slots):
            wanted = send_ref[slot, peer]
            out_ref[peer * slots + slot] = table_ref[jnp.where(wanted < 0, rows, wanted)]
        return carry

    lax.fori_loop(0, peers, fill, 0, unroll=2)
    put_own.wait()


def fold(value, low):
    top, bottom = value[0:HALF], value[HALF:]
    return jnp.where(low, top, swap_halves(bottom)), jnp.where(low, swap_halves(top), bottom)


def project_kernel(
    ghosts, source_ref, slot_ref, agg_ref, a_ref, p_ref, own_ref, sum_ref, tiles_hbm, meta_ref, count_ref,
    left_ref, first_ref, second_ref, odd_ref, even_tiles, odd_tiles, stage_ref,
    words_vec, words_ref, here_ref, done_ref, flying_ref, words_sem, sems,
):
    step = pl.program_id(0)
    last = pl.num_programs(0) - 1
    per_row, rows = source_ref.shape
    pairs = (per_row + 3) // 4 * 2
    sums = sum_ref.shape[0] // PIECES
    low_half, low_all = lane_low(HALF), lane_low(B)
    zero_all = jnp.zeros((B, LANES), jnp.bfloat16)

    @pl.when(step == 0)
    def _():
        source, slot = source_ref[...], slot_ref[...]
        part = (slot >= PS).astype(jnp.int32)
        for i in range(2, PIECES):
            part += (slot >= i * PS).astype(jnp.int32)
        place = agg_ref[...] * PS + slot - part * PS
        ghost = (source >= rows).astype(jnp.int32)
        words_vec[0] = (part * sums + place) * LIST + jnp.minimum(source, rows)
        words_vec[1] = jnp.maximum(source - rows, 0) * SPREAD + place
        words_vec[2] = part * 8 + ghost * 32
        load = pltpu.make_async_copy(words_vec, words_ref, words_sem)
        load.start()
        for i in range(PIECES):
            done_ref[i] = 0
            flying_ref[i] = 0

        def expand(i, carry):
            block = own_ref[i]
            turned = swap_halves(block)
            zero = jnp.zeros((HALF, LANES), jnp.bfloat16)
            first_ref[i, 0:HALF] = jnp.where(low_half, block, zero)
            first_ref[i, HALF:] = jnp.where(low_half, turned, zero)
            second_ref[i, 0:HALF] = jnp.where(low_half, zero, turned)
            second_ref[i, HALF:] = jnp.where(low_half, zero, block)
            return carry

        lax.fori_loop(0, rows, expand, 0, unroll=8)
        first_ref[rows] = zero_all
        second_ref[rows] = zero_all

        def clear(i, carry):
            for part in range(PIECES):
                sum_ref[part * sums + i] = jnp.zeros((HALF, LANES), jnp.float32)
                odd_ref[part * sums + i] = jnp.zeros((HALF, LANES), jnp.float32)
            return carry

        lax.fori_loop(0, sums, clear, 0, unroll=4)
        load.wait()

    flipped = p_ref[0].T
    row_of = lax.broadcasted_iota(jnp.int32, (B, KROWS), 1) % GROUP
    zero = jnp.zeros((B, KROWS), jnp.bfloat16)
    for r in range(GROUP):
        mine = row_of == r
        left_ref[r * B : (r + 1) * B, 0:KROWS] = jnp.where(mine, flipped[0:B], zero)
        left_ref[r * B : (r + 1) * B, KROWS:] = jnp.where(mine, flipped[B:], zero)
    low = lane_low(KROWS)

    def pair_of(pair):
        first = a_ref[2 * pair, 0]
        second = a_ref[min(2 * pair + 1, per_row - 1), 0]
        even = jnp.where(low, first, swap_halves(second))
        odd = jnp.where(low, swap_halves(first), second)
        return jnp.concatenate([even, odd], axis=0)

    counts = [jnp.int32(0), jnp.int32(0)]
    for pair in range(0, pairs, 2):
        right = jnp.concatenate([pair_of(pair), pair_of(pair + 1)], axis=1)
        both = jnp.dot(left_ref[...], right, preferred_element_type=jnp.float32).astype(jnp.bfloat16)
        for r in range(GROUP):
            row = step * GROUP + r
            moving = both[r * B : (r + 1) * B]
            weights, targets = [], []
            for h in range(2):
                tile = moving[:, h * LANES : (h + 1) * LANES]
                halves = []
                for parity, table, listed in ((0, first_ref, even_tiles), (1, second_ref, odd_tiles)):
                    k = 2 * (pair + h) + parity
                    if k >= per_row:
                        halves.append(zero_all)
                        targets.append(None)
                        continue
                    word = words_ref[0, k, row]
                    halves.append(table[word % LIST])
                    targets.append(word // LIST)
                    if k > 0:
                        flags = words_ref[2, k, row]
                        shift = flags % 32
                        at = (counts[parity] >> shift) % LIST + shift * (LIST // 8)
                        listed[at] = tile
                        here_ref[parity, at] = words_ref[1, k, row]
                        counts[parity] += (flags // 32) << shift
                filled = jnp.concatenate(halves, axis=0)
                blank = jnp.zeros_like(filled)
                weights.append(jnp.concatenate([filled, blank] if h == 0 else [blank, filled], axis=1))
            value = jnp.dot(moving, jnp.concatenate(weights, axis=0), preferred_element_type=jnp.float32)
            for h in range(2):
                even, odd = fold(value[:, h * LANES : (h + 1) * LANES], low_half)
                sum_ref[targets[2 * h]] += even
                if targets[2 * h + 1] is not None:
                    odd_ref[targets[2 * h + 1]] += odd

    no_entry = ghosts * SPREAD + sums
    for part in range(PIECES):
        even_count = (counts[0] >> (8 * part)) % LIST
        odd_count = (counts[1] >> (8 * part)) % LIST
        after = jnp.maximum(even_count, odd_count)
        before = done_ref[part]
        chunks = (after + CHUNK - 1) // CHUNK + jnp.where(step == last, 1, 0)

        def copy(i, start, part=part):
            return pltpu.make_async_copy(
                stage_ref.at[part, pl.ds(i * CHUNK, CHUNK)],
                tiles_hbm.at[part, pl.ds(start + i * CHUNK, CHUNK)],
                sems.at[part, i],
            )

        def finish(i, carry, copy=copy):
            copy(i, 0).wait()
            return carry

        lax.fori_loop(0, flying_ref[part], finish, 0)

        def merge(i, carry, part=part, even_count=even_count, odd_count=odd_count, before=before):
            end = part * LIST + jnp.minimum(i, LIST - 1)
            keep_even, keep_odd = i < even_count, i < odd_count
            even_at = jnp.where(low_all, i, LIST + CHUNK * 2) < even_count
            odd_at = jnp.where(low_all, LIST + CHUNK * 2, i) < odd_count
            tile = jnp.where(even_at, even_tiles[end], zero_all)
            stage_ref[part, i] = jnp.where(odd_at, odd_tiles[end], tile)
            meta_ref[2 * part, before + i] = jnp.where(keep_even, here_ref[0, end], no_entry)
            meta_ref[2 * part + 1, before + i] = jnp.where(keep_odd, here_ref[1, end], no_entry)
            return carry

        lax.fori_loop(0, jnp.where(step == last, chunks * CHUNK, after), merge, 0)

        def send(i, carry, copy=copy, before=before):
            copy(i, before).start()
            return carry

        lax.fori_loop(0, chunks, send, 0)
        flying_ref[part] = chunks
        done_ref[part] = before + after

    @pl.when(step == last)
    def _():
        def total(i, carry):
            for part in range(PIECES):
                sum_ref[part * sums + i] += odd_ref[part * sums + i]
            return carry

        lax.fori_loop(0, sums, total, 0, unroll=4)
        for part in range(PIECES):
            count_ref[part] = (done_ref[part] + CHUNK - 1) // CHUNK

            def drain(i, carry, part=part):
                pltpu.make_async_copy(
                    stage_ref.at[part, pl.ds(i * CHUNK, CHUNK)],
                    tiles_hbm.at[part, pl.ds(i * CHUNK, CHUNK)],
                    sems.at[part, i],
                ).wait()
                return carry

            lax.fori_loop(0, flying_ref[part], drain, 0)


def combine_kernel(
    part, meta_ref, count_ref, target_ref, ghost_ref, sum_hbm, tiles_hbm, out_ref,
    table_ref, even_ref, odd_ref, tiles_ref, bucket_ref, place_ref, per_peer_ref, sum_sem, sems,
):
    ghosts = ghost_ref.shape[0]
    coarse_here = target_ref.shape[0]
    sums = coarse_here * PS
    peers = out_ref.shape[0]
    chunks = count_ref[part]
    low_half, low_all = lane_low(HALF), lane_low(B)
    zero_all = jnp.zeros((B, LANES), jnp.bfloat16)
    load_sums = pltpu.make_async_copy(sum_hbm.at[pl.ds(part * sums, sums)], even_ref.at[pl.ds(0, sums)], sum_sem)
    load_sums.start()

    def fetch(i):
        slot = i % RING
        return pltpu.make_async_copy(tiles_hbm.at[part, pl.ds(i * CHUNK, CHUNK)], tiles_ref.at[slot], sems.at[slot])

    for i in range(RING - 1):

        @pl.when(i < chunks)
        def _():
            fetch(i).start()

    def expand(i, carry):
        block = ghost_ref[i]
        turned = swap_halves(block)
        table_ref[i, 0:HALF] = jnp.where(low_half, block, turned)
        table_ref[i, HALF:] = jnp.where(low_half, turned, block)
        return carry

    lax.fori_loop(0, ghosts, expand, 0, unroll=8)
    table_ref[ghosts] = zero_all

    def clear(i, carry):
        odd_ref[i] = jnp.zeros((HALF, LANES), jnp.float32)
        return carry

    lax.fori_loop(0, sums, clear, 0, unroll=8)

    for p in range(peers):
        per_peer_ref[p] = 0
        for q in range(CCAP):
            place_ref[p * CCAP + q] = -1

    def assign(c, carry):
        target = target_ref[c]
        peer = target // coarse_here % peers
        bucket = peer * CCAP + per_peer_ref[peer]
        per_peer_ref[peer] = per_peer_ref[peer] + 1
        bucket_ref[c] = bucket
        place_ref[bucket] = target % coarse_here
        return carry

    lax.fori_loop(0, coarse_here, assign, 0)
    payload = CCAP * PS * HALF
    second_slot = lax.broadcasted_iota(jnp.int32, (out_ref.shape[1] - payload, LANES), 1) // HALF % CCAP

    def note(p, carry):
        value = jnp.full(second_slot.shape, -1, jnp.int32)
        for q in range(CCAP):
            value = jnp.where(second_slot == q, place_ref[p * CCAP + q], value)
        out_ref[p, payload:] = value.astype(jnp.float32).astype(jnp.bfloat16)
        return carry

    lax.fori_loop(0, peers, note, 0)
    load_sums.wait()

    def work(i, carry):
        @pl.when(i + RING - 1 < chunks)
        def _():
            fetch(i + RING - 1).start()

        fetch(i).wait()
        slot = i % RING
        for j in range(0, CHUNK, 2):
            weights, targets = [], []
            for h in range(2):
                at = i * CHUNK + j + h
                even, odd = meta_ref[2 * part, at], meta_ref[2 * part + 1, at]
                upper = jnp.where(low_all, table_ref[even // SPREAD], zero_all)
                lower = jnp.where(low_all, zero_all, table_ref[odd // SPREAD])
                targets += [even % SPREAD, odd % SPREAD]
                filled = jnp.concatenate([upper, lower], axis=0)
                blank = jnp.zeros_like(filled)
                weights.append(jnp.concatenate([filled, blank] if h == 0 else [blank, filled], axis=1))
            moving = jnp.concatenate([tiles_ref[slot, j], tiles_ref[slot, j + 1]], axis=1)
            value = jnp.dot(moving, jnp.concatenate(weights, axis=0), preferred_element_type=jnp.float32)
            for h in range(2):
                even, odd = fold(value[:, h * LANES : (h + 1) * LANES], low_half)
                even_ref[targets[2 * h]] += even
                odd_ref[targets[2 * h + 1]] += odd
        return carry

    lax.fori_loop(0, chunks, work, 0)

    def finish(c, carry):
        bucket = bucket_ref[c]
        start = bucket % CCAP * (PS * HALF)
        for s in range(PS):
            total = even_ref[c * PS + s] + odd_ref[c * PS + s]
            here = pl.multiple_of(start + s * HALF, HALF)
            out_ref[bucket // CCAP, pl.ds(here, HALF)] = total.astype(jnp.bfloat16)
        return carry

    lax.fori_loop(0, coarse_here, finish, 0)


def place_kernel(in_ref, *rest):
    out_ref, from_ref = rest[-2:]
    step = pl.program_id(0)
    peers = in_ref.shape[0]
    per_step, groups = out_ref.shape[0], out_ref.shape[1]
    payload = CCAP * PS * HALF

    @pl.when(step == 0)
    def _():
        for p in range(peers):
            notes = in_ref[p, payload:].astype(jnp.float32)
            which = lax.broadcasted_iota(jnp.int32, notes.shape, 1) // HALF
            for q in range(CCAP):
                place = jnp.max(jnp.where(which == q, notes, -1.0)).astype(jnp.int32)

                @pl.when(place >= 0)
                def _():
                    from_ref[place] = p * CCAP + q

    perm = block_perm(True)
    low = lane_low(LANES)
    for i in range(per_step):
        s = step * per_step + i
        columns = []
        for g in range(groups):
            blocks = []
            for c in range(GROUP):
                bucket = from_ref[g * GROUP + c]
                here = pl.multiple_of((bucket % CCAP * PS + s) * HALF, HALF)
                blocks.append(in_ref[bucket // CCAP, pl.ds(here, HALF)])
            columns.append(jnp.concatenate(blocks, axis=0))
        moved = jnp.dot(perm, jnp.concatenate(columns, axis=1), preferred_element_type=jnp.float32)
        moved = moved.astype(jnp.bfloat16)
        for g in range(groups):
            mine = moved[:, g * LANES : (g + 1) * LANES]
            even, odd = mine[0:LANES], mine[LANES:]
            out_ref[i, g, 0:LANES] = jnp.where(low, even, swap_halves(odd))
            out_ref[i, g, LANES:] = jnp.where(low, swap_halves(even), odd)


def whole(shape):
    return pl.BlockSpec(shape, lambda *_: (0,) * len(shape))


def body(a_blocks, p_blocks, a_source, send_list, agg_local, coarse_slot, coarse_target):
    rows, per_row, _ = a_blocks.shape
    peers = lax.axis_size(("px", "py"))
    peers_y = lax.axis_size("py")
    slots = send_list.shape[2]
    coarse_here = rows // AGG
    groups = rows // GROUP
    pairs = (per_row + 3) // 4 * 2
    bf16 = jnp.bfloat16
    smem = pl.BlockSpec(memory_space=pltpu.SMEM)

    a_tiles = as_tiles(a_blocks.transpose(1, 0, 2))
    p_tiles = as_tiles(p_blocks)
    hbm = pl.BlockSpec(memory_space=pltpu.HBM)
    outgoing, own = pl.pallas_call(
        pack_kernel,
        in_specs=[hbm, hbm],
        out_specs=[whole((peers * slots, HALF, LANES)), hbm],
        out_shape=[
            jax.ShapeDtypeStruct((peers * slots, HALF, LANES), bf16),
            jax.ShapeDtypeStruct((rows, HALF, LANES), bf16),
        ],
        scratch_shapes=[
            pltpu.SMEM((slots, peers), jnp.int32),
            pltpu.VMEM((groups, KROWS, LANES), bf16),
            pltpu.VMEM((rows + 1, HALF, LANES), bf16),
            pltpu.SemaphoreType.DMA((groups // 2,)),
            pltpu.SemaphoreType.DMA,
            pltpu.SemaphoreType.DMA,
        ],
        compiler_params=pltpu.CompilerParams(vmem_limit_bytes=24 * MIB),
    )(send_list[0].T, p_tiles)
    arrived = lax.all_to_all(
        outgoing.reshape(peers, slots, HALF, LANES), ("px", "py"), split_axis=0, concat_axis=0, tiled=True
    ).reshape(peers * slots, HALF, LANES)

    sums = coarse_here * PS
    room = groups * LIST + STAGE
    local, tiles, meta, count = pl.pallas_call(
        functools.partial(project_kernel, peers * slots),
        grid=(groups,),
        in_specs=[
            whole((per_row, rows)),
            whole((per_row, rows)),
            whole((1, rows)),
            pl.BlockSpec((per_row, 1, KROWS, LANES), lambda g: (0, g, 0, 0)),
            pl.BlockSpec((1, KROWS, LANES), lambda g: (g, 0, 0)),
            whole((rows, HALF, LANES)),
        ],
        out_specs=[whole((PIECES * sums, HALF, LANES)), hbm, smem, smem],
        out_shape=[
            jax.ShapeDtypeStruct((PIECES * sums, HALF, LANES), jnp.float32),
            jax.ShapeDtypeStruct((PIECES, room, B, LANES), bf16),
            jax.ShapeDtypeStruct((2 * PIECES, room), jnp.int32),
            jax.ShapeDtypeStruct((PIECES,), jnp.int32),
        ],
        scratch_shapes=[
            pltpu.VMEM((GROUP * B, 2 * KROWS), bf16),
            pltpu.VMEM((rows + 1, B, LANES), bf16),
            pltpu.VMEM((rows + 1, B, LANES), bf16),
            pltpu.VMEM((PIECES * sums, HALF, LANES), jnp.float32),
            pltpu.VMEM((PIECES * LIST, B, LANES), bf16),
            pltpu.VMEM((PIECES * LIST, B, LANES), bf16),
            pltpu.VMEM((PIECES, STAGE, B, LANES), bf16),
            pltpu.VMEM((3, per_row, rows), jnp.int32),
            pltpu.SMEM((3, per_row, rows), jnp.int32),
            pltpu.SMEM((2, PIECES * LIST), jnp.int32),
            pltpu.SMEM((PIECES,), jnp.int32),
            pltpu.SMEM((PIECES,), jnp.int32),
            pltpu.SemaphoreType.DMA,
            pltpu.SemaphoreType.DMA((PIECES, STAGE // CHUNK)),
        ],
        compiler_params=pltpu.CompilerParams(vmem_limit_bytes=58 * MIB),
        cost_estimate=pl.CostEstimate(
            flops=4 * 512 * 512 * 128 * pairs * groups, bytes_accessed=45_000_000, transcendentals=0
        ),
    )(a_source.T, coarse_slot.T, agg_local.reshape(1, rows), a_tiles, p_tiles, own)

    piece_rows = CCAP * PS * HALF + 16
    received = []
    for part in range(PIECES):
        sent = pl.pallas_call(
            functools.partial(combine_kernel, part),
            in_specs=[smem, smem, smem, whole((peers * slots, HALF, LANES)), hbm, hbm],
            out_specs=whole((peers_y, piece_rows, LANES)),
            out_shape=jax.ShapeDtypeStruct((peers_y, piece_rows, LANES), bf16),
            scratch_shapes=[
                pltpu.VMEM((peers * slots + 1, B, LANES), bf16),
                pltpu.VMEM((sums + 1, HALF, LANES), jnp.float32),
                pltpu.VMEM((sums + 1, HALF, LANES), jnp.float32),
                pltpu.VMEM((RING, CHUNK, B, LANES), bf16),
                pltpu.SMEM((coarse_here,), jnp.int32),
                pltpu.SMEM((peers_y * CCAP,), jnp.int32),
                pltpu.SMEM((peers_y,), jnp.int32),
                pltpu.SemaphoreType.DMA,
                pltpu.SemaphoreType.DMA((RING,)),
            ],
            compiler_params=pltpu.CompilerParams(vmem_limit_bytes=16 * MIB + peers * slots * 28 * 1024),
            cost_estimate=pl.CostEstimate(flops=4_000_000_000, bytes_accessed=8_000_000, transcendentals=0),
        )(meta, count, coarse_target, arrived, local, tiles)
        received.append(lax.all_to_all(sent, "py", split_axis=0, concat_axis=0, tiled=True))

    per_step = 3
    out_groups = coarse_here // GROUP
    placed = None
    for part in range(PIECES):
        first = part * PS // per_step
        placed = pl.pallas_call(
            place_kernel,
            grid=(PS // per_step,),
            in_specs=[whole((peers_y, piece_rows, LANES))] + ([hbm] if part else []),
            out_specs=pl.BlockSpec((per_step, out_groups, KROWS, LANES), lambda s, first=first: (first + s, 0, 0, 0)),
            out_shape=jax.ShapeDtypeStruct((S, out_groups, KROWS, LANES), bf16),
            scratch_shapes=[pltpu.SMEM((coarse_here,), jnp.int32)],
            input_output_aliases={1: 0} if part else {},
            compiler_params=pltpu.CompilerParams(vmem_limit_bytes=24 * MIB),
            cost_estimate=pl.CostEstimate(flops=1_000_000_000, bytes_accessed=3_000_000, transcendentals=0),
        )(received[part], *([placed] if part else []))
    return from_tiles(placed).transpose(1, 0, 2)


def solution(mesh):
    rows = ("px", "py")
    in_specs = (
        P(rows, None, None),
        P(rows, None),
        P(rows, None),
        P(rows, None, None),
        P(rows),
        P(rows, None),
        P(rows),
    )
    return jax.shard_map(body, mesh=mesh, in_specs=in_specs, out_specs=P(rows, None, None), check_vma=False)
```

time: 143 us -> 176 us (1.23)
  blocking collectives: 46.4 us -> 0 us
  Pallas kernels: 84.4 us -> 122 us
  waiting for transfers between devices: 0.01 us -> 16.1 us
  local copies, waits for them, and re-layouts: 4.05 us -> 17.6 us
  starting transfers between devices: 7.3 us -> 19 us
    all_to_all x1 -> x0, blocking collectives: 46.4 us -> none  [body(): lax.all_to_all(sent, 'py', split_axis=0, concat_axis=0, tiled=True)]
    pallas_call x1, Pallas kernels: 53 us -> 78.1 us  [body(): pl.pallas_call(functools.partial(project_kernel, peers * slots), grid=(gr...]
    all_to_all x0 -> x3, waiting for transfers between devices: none -> 16.1 us  [body(): lax.all_to_all(sent, 'py', split_axis=0, concat_axis=0, tiled=True)]
    unnamed x8 -> x30, local copies, waits for them, and re-layouts: 4.05 us -> 17.6 us
    pallas_call x3 -> x7, Pallas kernels: 31.4 us -> 43.6 us  [the longest x3 30.4 us: body(): pl.pallas_call(functools.partial(combine_kernel, part), in_specs=[smem, s...]
    all_to_all x0 -> x3, starting transfers between devices: none -> 11.7 us  [body(): lax.all_to_all(sent, 'py', split_axis=0, concat_axis=0, tiled=True)]
  transfers between devices with their start and end apart: 1 -> 4, of which waited for: 0 -> 3; matrix products, arithmetic and copies ran while one was open for 0% -> 0% of each run, Pallas kernels for 37% -> 60%
where the time goes in v2:
time: 176 us; the launch traced here: 175 us
  Pallas kernels  122 us (69%)
  starting transfers between devices  19 us (11%)
  local copies, waits for them, and re-layouts  17.6 us (10%)
  waiting for transfers between devices  16.1 us (9%)
    pallas_call x1, Pallas kernels, body(): pl.pallas_call(functools.partial(project_kernel, peers * slots), grid=(gr...  78.1 us
    pallas_call x3, Pallas kernels, body(): pl.pallas_call(functools.partial(combine_kernel, part), in_specs=[smem, s...  30.4 us
    unnamed x30, local copies, waits for them, and re-layouts  17.6 us
    all_to_all x3, waiting for transfers between devices, body(): lax.all_to_all(sent, 'py', split_axis=0, concat_axis=0, tiled=True)  16.1 us
    all_to_all x3, starting transfers between devices, body(): lax.all_to_all(sent, 'py', split_axis=0, concat_axis=0, tiled=True)  11.7 us
    pallas_call x3, Pallas kernels, body(): pl.pallas_call(place_kernel, grid=(PS // per_step,), in_specs=[whole((pee...  9.75 us
    all_to_all x1, starting transfers between devices, body(): lax.all_to_all(outgoing.reshape(peers, slots, HALF, LANES), ('px', 'py'),...  7.29 us
  transfers between devices with their start and end apart: 4, of which 3 were waited for; matrix products, arithmetic and copies ran while one was open for 0% of the time, Pallas kernels for 60%

profile of v2, /device:TPU:0, one launch (start us, length us, event | category | flops | bytes accessed | tf_op | source)
XLA Modules:
  0.0 174.6 jit_solution(6679599753383307511)
XLA Ops:
  0.0 0.0 copy-start.7
  0.0 1.1 copy-done.7
  1.1 0.0 copy-start.13
  1.1 0.7 copy-done.13
  1.8 3.5 %shard_map.73 = (bf16[256,32,128]{2,1,0:T(8,128)(2,1)S(1)}, bf16[96,32,128]{2,1,0:T(8,128)(2,1)S(1)}) custom-call(s32[8,32]{1,0:T(8,128)S(1)} %bitcast.33, bf16[12,256,128]{2,1,0:T(8,128)(2,1)S(1)} %bitcast.32), custom_call_target="tpu_custom_call" | custom-call | tf_op jit(solution)/shard_map/pallas_call | solution.py:445
  5.3 0.0 copy-start.6
  5.3 1.3 copy-done.6
  6.6 0.0 copy-start.14
  6.6 0.9 copy-done.14
  7.5 7.3 %all-to-all-start = ((bf16[32,8,32,128]{3,2,1,0:T(8,128)(2,1)}), bf16[32,8,32,128]{3,2,1,0:T(8,128)(2,1)S(1)}, u32[]{:S(2)}, u32[]{:S(2)}) async-start(bf16[32,8,32,128]{3,2,1,0:T(8,128)(2,1)} %bitcast.30), calls=%async_computation | async-start | bytes 4194304 | tf_op jit(solution)/shard_map/all_to_all | solution.py:463
  14.8 0.0 copy-start.10
  14.8 78.1 %shard_map.74 = (f32[432,32,128]{2,1,0:T(8,128)}, bf16[3,1696,64,128]{3,2,1,0:T(8,128)(2,1)}, s32[6,1696]{1,0:T(8,128)}, s32[3]{0:T(128)}) custom-call(s32[27,96]{1,0:T(8,128)} %bitcast.35, s32[27,96]{1,0:T(8,128)} %bitcast.36, s32[1,96]{1,0:T(1,128)} %bitcast.37, bf16[27,12,256,128]{3,2,1,0:T(8,128)(2,1)} %bitcast.34, bf16[12,256,128]{2,1,0:T(8,128)(2,1)} %bitcast.31, ...), custom_call_target="tpu_custom_call" | custom-call | flops 22548578304 | bytes 45000000 | tf_op jit(solution)/shard_map/pallas_call | solution.py:469
  92.9 0.0 all-to-all-done
  92.9 0.0 copy-done.10
  93.0 0.0 copy-start
  93.0 3.0 %copy-done = f32[432,32,128]{2,1,0:T(8,128)S(1)} copy-done((f32[432,32,128]{2,1,0:T(8,128)S(1)}, f32[432,32,128]{2,1,0:T(8,128)}, u32[]{:S(2)}) %copy-start) | copy-done | bytes 7077912
  96.0 0.0 copy-start.8
  96.0 0.8 copy-done.8
  96.8 0.0 copy-start.11
  96.8 0.7 copy-done.11
  97.5 10.1 %shard_map.77 = bf16[8,592,128]{2,1,0:T(8,128)(2,1)S(1)} custom-call(s32[6,1696]{1,0:T(8,128)S(1)} %copy-done.8, s32[3]{0:T(128)S(1)} %copy-done.11, s32[16]{0:T(128)S(1)} %copy-done.10, bf16[256,32,128]{2,1,0:T(8,128)(2,1)S(1)} %bitcast.27, f32[432,32,128]{2,1,0:T(8,128)S(1)} %copy-done, bf16[3,1696,64,128]{3,2,1,0:T(8,128)(2,1)} %get-tuple-element.16.tiles_hbm), custom_call_target="tpu_custom_call" | custom-call | flops 4000000000 | bytes 8000000 | tf_op jit(solution)/shard_map/pallas_call | solution.py:512
  107.6 0.0 copy-start.5
  107.6 1.0 copy-done.5
  108.6 0.0 copy-start.9
  108.6 0.0 copy-start.12
  108.6 3.9 %all-to-all-start.3 = ((bf16[8,592,128]{2,1,0:T(8,128)(2,1)}), bf16[8,592,128]{2,1,0:T(8,128)(2,1)S(1)}, u32[]{:S(2)}, u32[]{:S(2)}) async-start(bf16[8,592,128]{2,1,0:T(8,128)(2,1)} %copy-done.5), calls=%async_computation.3 | async-start | bytes 2424832 | tf_op jit(solution)/shard_map/all_to_all | solution.py:531
  112.5 0.0 copy-done.9
  112.5 0.0 copy-done.12
  112.5 0.0 copy-start.1
  112.6 3.0 %copy-done.1 = f32[432,32,128]{2,1,0:T(8,128)S(1)} copy-done((f32[432,32,128]{2,1,0:T(8,128)S(1)}, f32[432,32,128]{2,1,0:T(8,128)}, u32[]{:S(2)}) %copy-start.1) | copy-done | bytes 7077912
  115.6 9.6 %shard_map.76 = bf16[8,592,128]{2,1,0:T(8,128)(2,1)S(1)} custom-call(s32[6,1696]{1,0:T(8,128)S(1)} %copy-done.9, s32[3]{0:T(128)S(1)} %copy-done.12, s32[16]{0:T(128)S(1)} %copy-done.10, bf16[256,32,128]{2,1,0:T(8,128)(2,1)S(1)} %bitcast.28, f32[432,32,128]{2,1,0:T(8,128)S(1)} %copy-done.1, bf16[3,1696,64,128]{3,2,1,0:T(8,128)(2,1)} %get-tuple-element.16.tiles_hbm), custom_call_target="tpu_custom_call" | custom-call | flops 4000000000 | bytes 8000000 | tf_op jit(solution)/shard_map/pallas_call | solution.py:512
  125.2 0.0 copy-start.4
  125.2 1.0 copy-done.4
  126.2 3.5 %all-to-all-done.3.in_ref = bf16[8,592,128]{2,1,0:T(8,128)(2,1)S(1)} async-done(((bf16[8,592,128]{2,1,0:T(8,128)(2,1)}), bf16[8,592,128]{2,1,0:T(8,128)(2,1)S(1)}, u32[]{:S(2)}, u32[]{:S(2)}) %all-to-all-start.3) | async-done | bytes 1212448 | tf_op jit(solution)/shard_map/all_to_all | solution.py:531
  129.7 4.3 %all-to-all-start.2 = ((bf16[8,592,128]{2,1,0:T(8,128)(2,1)}), bf16[8,592,128]{2,1,0:T(8,128)(2,1)}, u32[]{:S(2)}, u32[]{:S(2)}) async-start(bf16[8,592,128]{2,1,0:T(8,128)(2,1)} %copy-done.4), calls=%async_computation.2 | async-start | bytes 2424832 | tf_op jit(solution)/shard_map/all_to_all | solution.py:531
  134.0 0.0 copy-start.2
  134.0 3.0 %copy-done.2 = f32[432,32,128]{2,1,0:T(8,128)S(1)} copy-done((f32[432,32,128]{2,1,0:T(8,128)S(1)}, f32[432,32,128]{2,1,0:T(8,128)}, u32[]{:S(2)}) %copy-start.2) | copy-done | bytes 7077912
  137.0 10.6 %shard_map.75 = bf16[8,592,128]{2,1,0:T(8,128)(2,1)S(1)} custom-call(s32[6,1696]{1,0:T(8,128)S(1)} %copy-done.9, s32[3]{0:T(128)S(1)} %copy-done.12, s32[16]{0:T(128)S(1)} %copy-done.10, bf16[256,32,128]{2,1,0:T(8,128)(2,1)S(1)} %bitcast.29, f32[432,32,128]{2,1,0:T(8,128)S(1)} %copy-done.2, bf16[3,1696,64,128]{3,2,1,0:T(8,128)(2,1)} %get-tuple-element.16.tiles_hbm), custom_call_target="tpu_custom_call" | custom-call | flops 4000000000 | bytes 8000000 | tf_op jit(solution)/shard_map/pallas_call | solution.py:512
  147.6 0.0 copy-start.3
  147.6 1.1 copy-done.3
  148.7 2.4 %all-to-all-done.2.in_ref = bf16[8,592,128]{2,1,0:T(8,128)(2,1)} async-done(((bf16[8,592,128]{2,1,0:T(8,128)(2,1)}), bf16[8,592,128]{2,1,0:T(8,128)(2,1)}, u32[]{:S(2)}, u32[]{:S(2)}) %all-to-all-start.2) | async-done | bytes 1212448 | tf_op jit(solution)/shard_map/all_to_all | solution.py:531
  151.1 3.6 %all-to-all-start.1 = ((bf16[8,592,128]{2,1,0:T(8,128)(2,1)}), bf16[8,592,128]{2,1,0:T(8,128)(2,1)S(1)}, u32[]{:S(2)}, u32[]{:S(2)}) async-start(bf16[8,592,128]{2,1,0:T(8,128)(2,1)} %copy-done.3), calls=%async_computation.1 | async-start | bytes 2424832 | tf_op jit(solution)/shard_map/all_to_all | solution.py:531
  154.7 2.9 %shard_map.78.rest_0_ = bf16[27,2,256,128]{3,2,1,0:T(8,128)(2,1)} custom-call(bf16[8,592,128]{2,1,0:T(8,128)(2,1)S(1)} %all-to-all-done.3.in_ref), custom_call_target="tpu_custom_call" | custom-call | flops 1000000000 | bytes 3000000 | tf_op jit(solution)/shard_map/pallas_call | solution.py:538
  157.6 4.1 %shard_map.79.rest_0_ = bf16[27,2,256,128]{3,2,1,0:T(8,128)(2,1)} custom-call(bf16[8,592,128]{2,1,0:T(8,128)(2,1)} %all-to-all-done.2.in_ref, bf16[27,2,256,128]{3,2,1,0:T(8,128)(2,1)} %shard_map.78.rest_0_), custom_call_target="tpu_custom_call", output_to_operand_aliasing={{}: (1, {})} | custom-call | flops 1000000000 | bytes 3000000 | tf_op jit(solution)/shard_map/pallas_call | solution.py:538
  161.7 10.2 %all-to-all-done.1.in_ref = bf16[8,592,128]{2,1,0:T(8,128)(2,1)S(1)} async-done(((bf16[8,592,128]{2,1,0:T(8,128)(2,1)}), bf16[8,592,128]{2,1,0:T(8,128)(2,1)S(1)}, u32[]{:S(2)}, u32[]{:S(2)}) %all-to-all-start.1) | async-done | bytes 1212448 | tf_op jit(solution)/shard_map/all_to_all | solution.py:531
  171.8 2.8 %shard_map.80 = bf16[27,2,256,128]{3,2,1,0:T(8,128)(2,1)} custom-call(bf16[8,592,128]{2,1,0:T(8,128)(2,1)S(1)} %all-to-all-done.1.in_ref, bf16[27,2,256,128]{3,2,1,0:T(8,128)(2,1)} %shard_map.79.rest_0_), custom_call_target="tpu_custom_call", output_to_operand_aliasing={{}: (1, {})} | custom-call | flops 1000000000 | bytes 3000000 | tf_op jit(solution)/shard_map/pallas_call | solution.py:538
Async XLA Ops:
  0.0 1.1 copy-start.7
  1.1 0.7 copy-start.13
  5.3 1.3 copy-start.6
  6.6 0.9 copy-start.14
  7.5 85.4 %all-to-all-start = ((bf16[32,8,32,128]{3,2,1,0:T(8,128)(2,1)}), bf16[32,8,32,128]{3,2,1,0:T(8,128)(2,1)S(1)}, u32[]{:S(2)}, u32[]{:S(2)}) async-start(bf16[32,8,32,128]{3,2,1,0:T(8,128)(2,1)} %bitcast.30), calls=%async_computation | async-start | bytes 4194304 | tf_op jit(solution)/shard_map/all_to_all | solution.py:463
  14.8 78.1 %copy-start.10 = (s32[16]{0:T(128)S(1)}, s32[16]{0:T(128)}, u32[]{:S(2)}) copy-start(s32[16]{0:T(128)} %target_ref.5) | copy-start | bytes 196
  93.0 3.0 %copy-start = (f32[432,32,128]{2,1,0:T(8,128)S(1)}, f32[432,32,128]{2,1,0:T(8,128)}, u32[]{:S(2)}) copy-start(f32[432,32,128]{2,1,0:T(8,128)} %get-tuple-element.15.sum_hbm) | copy-start | bytes 21233668
  96.0 0.8 copy-start.8
  96.8 0.7 copy-start.11
  107.6 1.0 copy-start.5
  108.6 3.9 %copy-start.9 = (s32[6,1696]{1,0:T(8,128)S(1)}, s32[6,1696]{1,0:T(8,128)}, u32[]{:S(2)}) copy-start(s32[6,1696]{1,0:T(8,128)} %get-tuple-element.12.meta_ref) | copy-start | bytes 122116
  108.6 3.9 %copy-start.12 = (s32[3]{0:T(128)S(1)}, s32[3]{0:T(128)}, u32[]{:S(2)}) copy-start(s32[3]{0:T(128)} %get-tuple-element.13.count_ref) | copy-start | bytes 40
  108.6 21.1 %all-to-all-start.3 = ((bf16[8,592,128]{2,1,0:T(8,128)(2,1)}), bf16[8,592,128]{2,1,0:T(8,128)(2,1)S(1)}, u32[]{:S(2)}, u32[]{:S(2)}) async-start(bf16[8,592,128]{2,1,0:T(8,128)(2,1)} %copy-done.5), calls=%async_computation.3 | async-start | bytes 2424832 | tf_op jit(solution)/shard_map/all_to_all | solution.py:531
  112.5 3.0 %copy-start.1 = (f32[432,32,128]{2,1,0:T(8,128)S(1)}, f32[432,32,128]{2,1,0:T(8,128)}, u32[]{:S(2)}) copy-start(f32[432,32,128]{2,1,0:T(8,128)} %get-tuple-element.15.sum_hbm) | copy-start | bytes 21233668
  125.2 1.0 copy-start.4
  129.7 21.5 %all-to-all-start.2 = ((bf16[8,592,128]{2,1,0:T(8,128)(2,1)}), bf16[8,592,128]{2,1,0:T(8,128)(2,1)}, u32[]{:S(2)}, u32[]{:S(2)}) async-start(bf16[8,592,128]{2,1,0:T(8,128)(2,1)} %copy-done.4), calls=%async_computation.2 | async-start | bytes 2424832 | tf_op jit(solution)/shard_map/all_to_all | solution.py:531
  134.0 3.0 %copy-start.2 = (f32[432,32,128]{2,1,0:T(8,128)S(1)}, f32[432,32,128]{2,1,0:T(8,128)}, u32[]{:S(2)}) copy-start(f32[432,32,128]{2,1,0:T(8,128)} %get-tuple-element.15.sum_hbm) | copy-start | bytes 21233668
  147.6 1.1 copy-start.3
  151.1 20.7 %all-to-all-start.1 = ((bf16[8,592,128]{2,1,0:T(8,128)(2,1)}), bf16[8,592,128]{2,1,0:T(8,128)(2,1)S(1)}, u32[]{:S(2)}, u32[]{:S(2)}) async-start(bf16[8,592,128]{2,1,0:T(8,128)(2,1)} %copy-done.3), calls=%async_computation.1 | async-start | bytes 2424832 | tf_op jit(solution)/shard_map/all_to_all | solution.py:531

commit v3 on v2

--- a/solution.py
+++ b/solution.py
@@ -17,12 +17,15 @@
 GROUP = 8
 TILES = FLAT // LANES
 KROWS = GROUP * TILES
-PIECES = 3
+PIECES = 1
 PS = S // PIECES
-CHUNK = 16
+CHUNK = 32
+TURN = 8
 LIST = 128
 STAGE = LIST + 2 * CHUNK
-SPREAD = 1024
+SRC_BITS = 7
+PLACE_BITS = 10
+FLAG_BIT = 30
 RING = 4
 MIB = 1 << 20
 
@@ -127,9 +130,8 @@
             part += (slot >= i * PS).astype(jnp.int32)
         place = agg_ref[...] * PS + slot - part * PS
         ghost = (source >= rows).astype(jnp.int32)
-        words_vec[0] = (part * sums + place) * LIST + jnp.minimum(source, rows)
-        words_vec[1] = jnp.maximum(source - rows, 0) * SPREAD + place
-        words_vec[2] = part * 8 + ghost * 32
+        words_vec[0] = ((part * sums + place) << SRC_BITS) + jnp.minimum(source, rows)
+        words_vec[1] = (ghost << FLAG_BIT) + (jnp.maximum(source - rows, 0) << PLACE_BITS) + place
         load = pltpu.make_async_copy(words_vec, words_ref, words_sem)
         load.start()
         for i in range(PIECES):
@@ -193,15 +195,14 @@
                         targets.append(None)
                         continue
                     word = words_ref[0, k, row]
-                    halves.append(table[word % LIST])
-                    targets.append(word // LIST)
+                    halves.append(table[word & ((1 << SRC_BITS) - 1)])
+                    targets.append(word >> SRC_BITS)
                     if k > 0:
-                        flags = words_ref[2, k, row]
-                        shift = flags % 32
-                        at = (counts[parity] >> shift) % LIST + shift * (LIST // 8)
+                        at = counts[parity]
+                        note = words_ref[1, k, row]
                         listed[at] = tile
-                        here_ref[parity, at] = words_ref[1, k, row]
-                        counts[parity] += (flags // 32) << shift
+                        here_ref[parity, at] = note
+                        counts[parity] = at + (note >> FLAG_BIT)
                 filled = jnp.concatenate(halves, axis=0)
                 blank = jnp.zeros_like(filled)
                 weights.append(jnp.concatenate([filled, blank] if h == 0 else [blank, filled], axis=1))
@@ -212,13 +213,12 @@
                 if targets[2 * h + 1] is not None:
                     odd_ref[targets[2 * h + 1]] += odd
 
-    no_entry = ghosts * SPREAD + sums
+    no_entry = (ghosts << PLACE_BITS) + sums
     for part in range(PIECES):
-        even_count = (counts[0] >> (8 * part)) % LIST
-        odd_count = (counts[1] >> (8 * part)) % LIST
+        even_count, odd_count = counts
         after = jnp.maximum(even_count, odd_count)
         before = done_ref[part]
-        chunks = (after + CHUNK - 1) // CHUNK + jnp.where(step == last, 1, 0)
+        chunks = lax.div(after + CHUNK - 1, CHUNK) + jnp.where(step == last, 1, 0)
 
         def copy(i, start, part=part):
             return pltpu.make_async_copy(
@@ -233,18 +233,20 @@
 
         lax.fori_loop(0, flying_ref[part], finish, 0)
 
-        def merge(i, carry, part=part, even_count=even_count, odd_count=odd_count, before=before):
-            end = part * LIST + jnp.minimum(i, LIST - 1)
-            keep_even, keep_odd = i < even_count, i < odd_count
-            even_at = jnp.where(low_all, i, LIST + CHUNK * 2) < even_count
-            odd_at = jnp.where(low_all, LIST + CHUNK * 2, i) < odd_count
-            tile = jnp.where(even_at, even_tiles[end], zero_all)
-            stage_ref[part, i] = jnp.where(odd_at, odd_tiles[end], tile)
-            meta_ref[2 * part, before + i] = jnp.where(keep_even, here_ref[0, end], no_entry)
-            meta_ref[2 * part + 1, before + i] = jnp.where(keep_odd, here_ref[1, end], no_entry)
+        def merge(turn, carry, part=part, even_count=even_count, odd_count=odd_count, before=before):
+            for j in range(TURN):
+                i = turn * TURN + j
+                end = part * LIST + jnp.minimum(i, LIST - 1)
+                even_at = jnp.where(low_all, i, STAGE) < even_count
+                odd_at = jnp.where(low_all, STAGE, i) < odd_count
+                tile = jnp.where(even_at, even_tiles[end], zero_all)
+                stage_ref[part, i] = jnp.where(odd_at, odd_tiles[end], tile)
+                meta_ref[2 * part, before + i] = jnp.where(i < even_count, here_ref[0, end], no_entry)
+                meta_ref[2 * part + 1, before + i] = jnp.where(i < odd_count, here_ref[1, end], no_entry)
             return carry
 
-        lax.fori_loop(0, jnp.where(step == last, chunks * CHUNK, after), merge, 0)
+        turns = jnp.where(step == last, chunks * (CHUNK // TURN), (after + TURN - 1) >> 3)
+        lax.fori_loop(0, turns, merge, 0)
 
         def send(i, carry, copy=copy, before=before):
             copy(i, before).start()
@@ -263,7 +265,7 @@
 
         lax.fori_loop(0, sums, total, 0, unroll=4)
         for part in range(PIECES):
-            count_ref[part] = (done_ref[part] + CHUNK - 1) // CHUNK
+            count_ref[part] = lax.div(done_ref[part] + CHUNK - 1, CHUNK)
 
             def drain(i, carry, part=part):
                 pltpu.make_async_copy(
@@ -291,7 +293,7 @@
     load_sums.start()
 
     def fetch(i):
-        slot = i % RING
+        slot = lax.rem(i, RING)
         return pltpu.make_async_copy(tiles_hbm.at[part, pl.ds(i * CHUNK, CHUNK)], tiles_ref.at[slot], sems.at[slot])
 
     for i in range(RING - 1):
@@ -323,11 +325,11 @@
 
     def assign(c, carry):
         target = target_ref[c]
-        peer = target // coarse_here % peers
+        peer = lax.rem(lax.div(target, coarse_here), peers)
         bucket = peer * CCAP + per_peer_ref[peer]
         per_peer_ref[peer] = per_peer_ref[peer] + 1
         bucket_ref[c] = bucket
-        place_ref[bucket] = target % coarse_here
+        place_ref[bucket] = lax.rem(target, coarse_here)
         return carry
 
     lax.fori_loop(0, coarse_here, assign, 0)
@@ -350,15 +352,15 @@
             fetch(i + RING - 1).start()
 
         fetch(i).wait()
-        slot = i % RING
+        slot = lax.rem(i, RING)
         for j in range(0, CHUNK, 2):
             weights, targets = [], []
             for h in range(2):
                 at = i * CHUNK + j + h
                 even, odd = meta_ref[2 * part, at], meta_ref[2 * part + 1, at]
-                upper = jnp.where(low_all, table_ref[even // SPREAD], zero_all)
-                lower = jnp.where(low_all, zero_all, table_ref[odd // SPREAD])
-                targets += [even % SPREAD, odd % SPREAD]
+                upper = jnp.where(low_all, table_ref[(even >> PLACE_BITS) & ((1 << FLAG_BIT - PLACE_BITS) - 1)], zero_all)
+                lower = jnp.where(low_all, zero_all, table_ref[(odd >> PLACE_BITS) & ((1 << FLAG_BIT - PLACE_BITS) - 1)])
+                targets += [even & ((1 << PLACE_BITS) - 1), odd & ((1 << PLACE_BITS) - 1)]
                 filled = jnp.concatenate([upper, lower], axis=0)
                 blank = jnp.zeros_like(filled)
                 weights.append(jnp.concatenate([filled, blank] if h == 0 else [blank, filled], axis=1))
@@ -385,7 +387,7 @@
 
 
 def place_kernel(in_ref, *rest):
-    out_ref, from_ref = rest[-2:]
+    out_ref, peer_ref, start_ref = rest[-3:]
     step = pl.program_id(0)
     peers = in_ref.shape[0]
     per_step, groups = out_ref.shape[0], out_ref.shape[1]
@@ -401,7 +403,8 @@
 
                 @pl.when(place >= 0)
                 def _():
-                    from_ref[place] = p * CCAP + q
+                    peer_ref[place] = p
+                    start_ref[place] = q * PS * HALF
 
     perm = block_perm(True)
     low = lane_low(LANES)
@@ -411,9 +414,9 @@
         for g in range(groups):
             blocks = []
             for c in range(GROUP):
-                bucket = from_ref[g * GROUP + c]
-                here = pl.multiple_of((bucket % CCAP * PS + s) * HALF, HALF)
-                blocks.append(in_ref[bucket // CCAP, pl.ds(here, HALF)])
+                row = g * GROUP + c
+                here = pl.multiple_of(start_ref[row] + s * HALF, HALF)
+                blocks.append(in_ref[peer_ref[row], pl.ds(here, HALF)])
             columns.append(jnp.concatenate(blocks, axis=0))
         moved = jnp.dot(perm, jnp.concatenate(columns, axis=1), preferred_element_type=jnp.float32)
         moved = moved.astype(jnp.bfloat16)
@@ -458,7 +461,7 @@
             pltpu.SemaphoreType.DMA,
             pltpu.SemaphoreType.DMA,
         ],
-        compiler_params=pltpu.CompilerParams(vmem_limit_bytes=24 * MIB),
+        compiler_params=pltpu.CompilerParams(vmem_limit_bytes=60 * MIB),
     )(send_list[0].T, p_tiles)
     arrived = lax.all_to_all(
         outgoing.reshape(peers, slots, HALF, LANES), ("px", "py"), split_axis=0, concat_axis=0, tiled=True
@@ -492,8 +495,8 @@
             pltpu.VMEM((PIECES * LIST, B, LANES), bf16),
             pltpu.VMEM((PIECES * LIST, B, LANES), bf16),
             pltpu.VMEM((PIECES, STAGE, B, LANES), bf16),
-            pltpu.VMEM((3, per_row, rows), jnp.int32),
-            pltpu.SMEM((3, per_row, rows), jnp.int32),
+            pltpu.VMEM((2, per_row, rows), jnp.int32),
+            pltpu.SMEM((2, per_row, rows), jnp.int32),
             pltpu.SMEM((2, PIECES * LIST), jnp.int32),
             pltpu.SMEM((PIECES,), jnp.int32),
             pltpu.SMEM((PIECES,), jnp.int32),
@@ -525,7 +528,7 @@
                 pltpu.SemaphoreType.DMA,
                 pltpu.SemaphoreType.DMA((RING,)),
             ],
-            compiler_params=pltpu.CompilerParams(vmem_limit_bytes=16 * MIB + peers * slots * 28 * 1024),
+            compiler_params=pltpu.CompilerParams(vmem_limit_bytes=56 * MIB),
             cost_estimate=pl.CostEstimate(flops=4_000_000_000, bytes_accessed=8_000_000, transcendentals=0),
         )(meta, count, coarse_target, arrived, local, tiles)
         received.append(lax.all_to_all(sent, "py", split_axis=0, concat_axis=0, tiled=True))
@@ -541,7 +544,7 @@
             in_specs=[whole((peers_y, piece_rows, LANES))] + ([hbm] if part else []),
             out_specs=pl.BlockSpec((per_step, out_groups, KROWS, LANES), lambda s, first=first: (first + s, 0, 0, 0)),
             out_shape=jax.ShapeDtypeStruct((S, out_groups, KROWS, LANES), bf16),
-            scratch_shapes=[pltpu.SMEM((coarse_here,), jnp.int32)],
+            scratch_shapes=[pltpu.SMEM((coarse_here,), jnp.int32), pltpu.SMEM((coarse_here,), jnp.int32)],
             input_output_aliases={1: 0} if part else {},
             compiler_params=pltpu.CompilerParams(vmem_limit_bytes=24 * MIB),
             cost_estimate=pl.CostEstimate(flops=1_000_000_000, bytes_accessed=3_000_000, transcendentals=0),

time: 176 us -> 131 us (0.74)
  Pallas kernels: 122 us -> 71.8 us
  blocking collectives: 0 us -> 46 us
  local copies, waits for them, and re-layouts: 17.6 us -> 1.32 us
  waiting for transfers between devices: 16.1 us -> 3.53 us
  starting transfers between devices: 19 us -> 7.3 us
    all_to_all x0 -> x1, blocking collectives: none -> 46 us  [body(): lax.all_to_all(sent, 'py', split_axis=0, concat_axis=0, tiled=True)]
    pallas_call x1, Pallas kernels: 78.1 us -> 45.4 us  [body(): pl.pallas_call(functools.partial(project_kernel, peers * slots), grid=(gr...]
    unnamed x30 -> x2, local copies, waits for them, and re-layouts: 17.6 us -> 1.32 us
    all_to_all x3 -> x0, waiting for transfers between devices: 16.1 us -> none  [body(): lax.all_to_all(sent, 'py', split_axis=0, concat_axis=0, tiled=True)]
    pallas_call x3 -> x1, Pallas kernels: 30.4 us -> 15.7 us  [body(): pl.pallas_call(functools.partial(combine_kernel, part), in_specs=[smem, s...]
    all_to_all x3 -> x0, starting transfers between devices: 11.7 us -> none  [body(): lax.all_to_all(sent, 'py', split_axis=0, concat_axis=0, tiled=True)]
    pallas_call x3 -> x1, Pallas kernels: 9.75 us -> 5.81 us  [body(): pl.pallas_call(place_kernel, grid=(PS // per_step,), in_specs=[whole((pee...]
    all_to_all x1, waiting for transfers between devices: 0.01 us -> 3.53 us  [body(): lax.all_to_all(outgoing.reshape(peers, slots, HALF, LANES), ('px', 'py'),...]
  transfers between devices with their start and end apart: 4 -> 1, of which waited for: 3 -> 1; matrix products, arithmetic and copies ran while one was open for 0% -> 0% of each run, Pallas kernels for 60% -> 35%
where the time goes in v3:
time: 131 us; the launch traced here: 130 us
  Pallas kernels  71.8 us (55%)
  blocking collectives  46 us (35%)
  starting transfers between devices  7.3 us (6%)
  waiting for transfers between devices  3.53 us (3%)
  local copies, waits for them, and re-layouts  1.32 us (1%)
    all_to_all x1, blocking collectives, body(): lax.all_to_all(sent, 'py', split_axis=0, concat_axis=0, tiled=True)  46 us
    pallas_call x1, Pallas kernels, body(): pl.pallas_call(functools.partial(project_kernel, peers * slots), grid=(gr...  45.4 us
    pallas_call x1, Pallas kernels, body(): pl.pallas_call(functools.partial(combine_kernel, part), in_specs=[smem, s...  15.7 us
    all_to_all x1, starting transfers between devices, body(): lax.all_to_all(outgoing.reshape(peers, slots, HALF, LANES), ('px', 'py'),...  7.3 us
    pallas_call x1, Pallas kernels, body(): pl.pallas_call(place_kernel, grid=(PS // per_step,), in_specs=[whole((pee...  5.81 us
    pallas_call x1, Pallas kernels, body(): pl.pallas_call(pack_kernel, in_specs=[hbm, hbm], out_specs=[whole((peers...  4.92 us
    all_to_all x1, waiting for transfers between devices, body(): lax.all_to_all(outgoing.reshape(peers, slots, HALF, LANES), ('px', 'py'),...  3.53 us
  transfers between devices with their start and end apart: 1, of which 1 were waited for; matrix products, arithmetic and copies ran while one was open for 0% of the time, Pallas kernels for 35%

profile of v3, /device:TPU:0, one launch (start us, length us, event | category | flops | bytes accessed | tf_op | source)
XLA Modules:
  0.0 130.0 jit_solution(13425171990027550344)
XLA Ops:
  0.0 4.9 %shard_map.73 = (bf16[256,32,128]{2,1,0:T(8,128)(2,1)}, bf16[96,32,128]{2,1,0:T(8,128)(2,1)}) custom-call(s32[8,32]{1,0:T(8,128)} %bitcast.31, bf16[12,256,128]{2,1,0:T(8,128)(2,1)} %bitcast.29), custom_call_target="tpu_custom_call" | custom-call | tf_op jit(solution)/shard_map/pallas_call | solution.py:448
  4.9 7.3 %all-to-all-start = ((bf16[32,8,32,128]{3,2,1,0:T(8,128)(2,1)}), bf16[32,8,32,128]{3,2,1,0:T(8,128)(2,1)S(1)}, u32[]{:S(2)}, u32[]{:S(2)}) async-start(bf16[32,8,32,128]{3,2,1,0:T(8,128)(2,1)} %bitcast.28), calls=%async_computation | async-start | bytes 4194304 | tf_op jit(solution)/shard_map/all_to_all | solution.py:466
  12.2 45.4 %shard_map.74 = (f32[432,32,128]{2,1,0:T(8,128)}, bf16[1,1728,64,128]{3,2,1,0:T(8,128)(2,1)}, s32[2,1728]{1,0:T(2,128)}, s32[1]{0:T(128)}) custom-call(s32[27,96]{1,0:T(8,128)} %bitcast.33, s32[27,96]{1,0:T(8,128)} %bitcast.34, s32[1,96]{1,0:T(1,128)} %bitcast.35, bf16[27,12,256,128]{3,2,1,0:T(8,128)(2,1)} %bitcast.32, bf16[12,256,128]{2,1,0:T(8,128)(2,1)} %bitcast.30, ...), custom_call_target="tpu_custom_call" | custom-call | flops 22548578304 | bytes 45000000 | tf_op jit(solution)/shard_map/pallas_call | solution.py:472
  57.6 3.5 %all-to-all-done = bf16[32,8,32,128]{3,2,1,0:T(8,128)(2,1)S(1)} async-done(((bf16[32,8,32,128]{3,2,1,0:T(8,128)(2,1)}), bf16[32,8,32,128]{3,2,1,0:T(8,128)(2,1)S(1)}, u32[]{:S(2)}, u32[]{:S(2)}) %all-to-all-start) | async-done | bytes 2097184 | tf_op jit(solution)/shard_map/all_to_all | solution.py:466
  61.1 0.0 copy-start
  61.1 1.3 %copy-done = bf16[32,8,32,128]{3,2,1,0:T(8,128)(2,1)} copy-done((bf16[32,8,32,128]{3,2,1,0:T(8,128)(2,1)}, bf16[32,8,32,128]{3,2,1,0:T(8,128)(2,1)S(1)}, u32[]{:S(2)}) %copy-start) | copy-done | bytes 2097176
  62.5 15.7 %shard_map.75 = bf16[8,1744,128]{2,1,0:T(8,128)(2,1)} custom-call(s32[2,1728]{1,0:T(2,128)} %get-tuple-element.12.meta_ref, s32[1]{0:T(128)} %get-tuple-element.13.count_ref, s32[16]{0:T(128)} %target_ref.1, bf16[256,32,128]{2,1,0:T(8,128)(2,1)} %bitcast.27, f32[432,32,128]{2,1,0:T(8,128)} %get-tuple-element.15.sum_hbm, ...), custom_call_target="tpu_custom_call" | custom-call | flops 4000000000 | bytes 8000000 | tf_op jit(solution)/shard_map/pallas_call | solution.py:515
  78.2 46.0 %all_to_all.10.in_ref = bf16[8,1744,128]{2,1,0:T(8,128)(2,1)S(1)} all-to-all(bf16[8,1744,128]{2,1,0:T(8,128)(2,1)} %shard_map.75), channel_id=1, replica_groups=mesh['px'=4,'py'=8] {'py'}, dimensions={0} | all-to-all | bytes 7143424 | tf_op jit(solution)/shard_map/all_to_all | solution.py:534
  124.2 5.8 %shard_map.76 = bf16[27,2,256,128]{3,2,1,0:T(8,128)(2,1)} custom-call(bf16[8,1744,128]{2,1,0:T(8,128)(2,1)S(1)} %all_to_all.10.in_ref), custom_call_target="tpu_custom_call" | custom-call | flops 1000000000 | bytes 3000000 | tf_op jit(solution)/shard_map/pallas_call | solution.py:541
Async XLA Ops:
  4.9 56.2 %all-to-all-start = ((bf16[32,8,32,128]{3,2,1,0:T(8,128)(2,1)}), bf16[32,8,32,128]{3,2,1,0:T(8,128)(2,1)S(1)}, u32[]{:S(2)}, u32[]{:S(2)}) async-start(bf16[32,8,32,128]{3,2,1,0:T(8,128)(2,1)} %bitcast.28), calls=%async_computation | async-start | bytes 4194304 | tf_op jit(solution)/shard_map/all_to_all | solution.py:466
  61.1 1.3 %copy-start = (bf16[32,8,32,128]{3,2,1,0:T(8,128)(2,1)}, bf16[32,8,32,128]{3,2,1,0:T(8,128)(2,1)S(1)}, u32[]{:S(2)}) copy-start(bf16[32,8,32,128]{3,2,1,0:T(8,128)(2,1)S(1)} %all-to-all-done) | copy-start | bytes 6291460

commit v4 on v3

--- a/solution.py
+++ b/solution.py
@@ -20,6 +20,7 @@
 PIECES = 1
 PS = S // PIECES
 CHUNK = 32
+PEERS = 8
 TURN = 8
 LIST = 128
 STAGE = LIST + 2 * CHUNK
@@ -61,7 +62,9 @@
     return jnp.where(same_r & same_j, 1.0, 0.0).astype(jnp.bfloat16)
 
 
-def pack_kernel(send_hbm, p_hbm, out_ref, own_hbm, send_ref, p_ref, table_ref, sems, send_sem, own_sem):
+def pack_kernel(
+    send_hbm, p_hbm, out_hbm, own_hbm, send_ref, p_ref, table_ref, out_ref, sems, send_sem, own_sem, out_sems
+):
     groups = p_ref.shape[0]
     rows = groups * GROUP
     slots, peers = send_ref.shape
@@ -100,8 +103,16 @@
             out_ref[peer * slots + slot] = table_ref[jnp.where(wanted < 0, rows, wanted)]
         return carry
 
-    lax.fori_loop(0, peers, fill, 0, unroll=2)
+    def put(i):
+        span = pl.ds(i * PEERS * slots, PEERS * slots)
+        return pltpu.make_async_copy(out_ref.at[span], out_hbm.at[span], out_sems.at[i])
+
+    for i in range(peers // PEERS):
+        lax.fori_loop(i * PEERS, (i + 1) * PEERS, fill, 0, unroll=2)
+        put(i).start()
     put_own.wait()
+    for i in range(peers // PEERS):
+        put(i).wait()
 
 
 def fold(value, low):
@@ -279,18 +290,21 @@
 
 
 def combine_kernel(
-    part, meta_ref, count_ref, target_ref, ghost_ref, sum_hbm, tiles_hbm, out_ref,
-    table_ref, even_ref, odd_ref, tiles_ref, bucket_ref, place_ref, per_peer_ref, sum_sem, sems,
+    part, meta_ref, count_ref, target_ref, ghost_hbm, sum_hbm, tiles_hbm, out_hbm,
+    ghost_ref, even_ref, odd_ref, tiles_ref, out_ref, bucket_ref, place_ref, per_peer_ref,
+    ghost_sem, sum_sem, note_sem, sems, out_sems,
 ):
-    ghosts = ghost_ref.shape[0]
+    ghosts = ghost_hbm.shape[0]
     coarse_here = target_ref.shape[0]
     sums = coarse_here * PS
     peers = out_ref.shape[0]
     chunks = count_ref[part]
-    low_half, low_all = lane_low(HALF), lane_low(B)
-    zero_all = jnp.zeros((B, LANES), jnp.bfloat16)
+    low_half = lane_low(HALF)
+    zero_half = jnp.zeros((HALF, LANES), jnp.bfloat16)
     load_sums = pltpu.make_async_copy(sum_hbm.at[pl.ds(part * sums, sums)], even_ref.at[pl.ds(0, sums)], sum_sem)
     load_sums.start()
+    load_ghosts = pltpu.make_async_copy(ghost_hbm, ghost_ref.at[pl.ds(0, ghosts)], ghost_sem)
+    load_ghosts.start()
 
     def fetch(i):
         slot = lax.rem(i, RING)
@@ -302,15 +316,7 @@
         def _():
             fetch(i).start()
 
-    def expand(i, carry):
-        block = ghost_ref[i]
-        turned = swap_halves(block)
-        table_ref[i, 0:HALF] = jnp.where(low_half, block, turned)
-        table_ref[i, HALF:] = jnp.where(low_half, turned, block)
-        return carry
-
-    lax.fori_loop(0, ghosts, expand, 0, unroll=8)
-    table_ref[ghosts] = zero_all
+    ghost_ref[ghosts] = zero_half
 
     def clear(i, carry):
         odd_ref[i] = jnp.zeros((HALF, LANES), jnp.float32)
@@ -344,6 +350,10 @@
         return carry
 
     lax.fori_loop(0, peers, note, 0)
+    notes = pl.ds(payload, out_ref.shape[1] - payload)
+    put_notes = pltpu.make_async_copy(out_ref.at[:, notes], out_hbm.at[:, notes], note_sem)
+    put_notes.start()
+    load_ghosts.wait()
     load_sums.wait()
 
     def work(i, carry):
@@ -358,10 +368,18 @@
             for h in range(2):
                 at = i * CHUNK + j + h
                 even, odd = meta_ref[2 * part, at], meta_ref[2 * part + 1, at]
-                upper = jnp.where(low_all, table_ref[(even >> PLACE_BITS) & ((1 << FLAG_BIT - PLACE_BITS) - 1)], zero_all)
-                lower = jnp.where(low_all, zero_all, table_ref[(odd >> PLACE_BITS) & ((1 << FLAG_BIT - PLACE_BITS) - 1)])
+                first = ghost_ref[(even >> PLACE_BITS) & ((1 << FLAG_BIT - PLACE_BITS) - 1)]
+                second = ghost_ref[(odd >> PLACE_BITS) & ((1 << FLAG_BIT - PLACE_BITS) - 1)]
                 targets += [even & ((1 << PLACE_BITS) - 1), odd & ((1 << PLACE_BITS) - 1)]
-                filled = jnp.concatenate([upper, lower], axis=0)
+                filled = jnp.concatenate(
+                    [
+                        jnp.where(low_half, first, zero_half),
+                        jnp.where(low_half, swap_halves(first), zero_half),
+                        jnp.where(low_half, zero_half, swap_halves(second)),
+                        jnp.where(low_half, zero_half, second),
+                    ],
+                    axis=0,
+                )
                 blank = jnp.zeros_like(filled)
                 weights.append(jnp.concatenate([filled, blank] if h == 0 else [blank, filled], axis=1))
             moving = jnp.concatenate([tiles_ref[slot, j], tiles_ref[slot, j + 1]], axis=1)
@@ -374,16 +392,27 @@
 
     lax.fori_loop(0, chunks, work, 0)
 
+    def put(c):
+        bucket = bucket_ref[c]
+        span = pl.ds(pl.multiple_of(lax.rem(bucket, CCAP) * (PS * HALF), HALF), PS * HALF)
+        peer = lax.div(bucket, CCAP)
+        return pltpu.make_async_copy(out_ref.at[peer, span], out_hbm.at[peer, span], out_sems.at[c])
+
     def finish(c, carry):
         bucket = bucket_ref[c]
-        start = bucket % CCAP * (PS * HALF)
+        start = lax.rem(bucket, CCAP) * (PS * HALF)
+        peer = lax.div(bucket, CCAP)
+        first = c * PS
         for s in range(PS):
-            total = even_ref[c * PS + s] + odd_ref[c * PS + s]
+            total = even_ref[first + s] + odd_ref[first + s]
             here = pl.multiple_of(start + s * HALF, HALF)
-            out_ref[bucket // CCAP, pl.ds(here, HALF)] = total.astype(jnp.bfloat16)
+            out_ref[peer, pl.ds(here, HALF)] = total.astype(jnp.bfloat16)
+        put(c).start()
         return carry
 
     lax.fori_loop(0, coarse_here, finish, 0)
+    put_notes.wait()
+    lax.fori_loop(0, coarse_here, lambda c, carry: (put(c).wait(), carry)[1], 0)
 
 
 def place_kernel(in_ref, *rest):
@@ -400,11 +429,9 @@
             which = lax.broadcasted_iota(jnp.int32, notes.shape, 1) // HALF
             for q in range(CCAP):
                 place = jnp.max(jnp.where(which == q, notes, -1.0)).astype(jnp.int32)
-
-                @pl.when(place >= 0)
-                def _():
-                    peer_ref[place] = p
-                    start_ref[place] = q * PS * HALF
+                entry = jnp.where(place < 0, groups * GROUP, place)
+                peer_ref[entry] = p
+                start_ref[entry] = q * PS * HALF
 
     perm = block_perm(True)
     low = lane_low(LANES)
@@ -448,7 +475,7 @@
     outgoing, own = pl.pallas_call(
         pack_kernel,
         in_specs=[hbm, hbm],
-        out_specs=[whole((peers * slots, HALF, LANES)), hbm],
+        out_specs=[hbm, hbm],
         out_shape=[
             jax.ShapeDtypeStruct((peers * slots, HALF, LANES), bf16),
             jax.ShapeDtypeStruct((rows, HALF, LANES), bf16),
@@ -457,9 +484,11 @@
             pltpu.SMEM((slots, peers), jnp.int32),
             pltpu.VMEM((groups, KROWS, LANES), bf16),
             pltpu.VMEM((rows + 1, HALF, LANES), bf16),
+            pltpu.VMEM((peers * slots, HALF, LANES), bf16),
             pltpu.SemaphoreType.DMA((groups // 2,)),
             pltpu.SemaphoreType.DMA,
             pltpu.SemaphoreType.DMA,
+            pltpu.SemaphoreType.DMA((peers // PEERS,)),
         ],
         compiler_params=pltpu.CompilerParams(vmem_limit_bytes=60 * MIB),
     )(send_list[0].T, p_tiles)
@@ -503,7 +532,7 @@
             pltpu.SemaphoreType.DMA,
             pltpu.SemaphoreType.DMA((PIECES, STAGE // CHUNK)),
         ],
-        compiler_params=pltpu.CompilerParams(vmem_limit_bytes=58 * MIB),
+        compiler_params=pltpu.CompilerParams(vmem_limit_bytes=63 * MIB),
         cost_estimate=pl.CostEstimate(
             flops=4 * 512 * 512 * 128 * pairs * groups, bytes_accessed=45_000_000, transcendentals=0
         ),
@@ -514,26 +543,30 @@
     for part in range(PIECES):
         sent = pl.pallas_call(
             functools.partial(combine_kernel, part),
-            in_specs=[smem, smem, smem, whole((peers * slots, HALF, LANES)), hbm, hbm],
-            out_specs=whole((peers_y, piece_rows, LANES)),
+            in_specs=[smem, smem, smem, hbm, hbm, hbm],
+            out_specs=hbm,
             out_shape=jax.ShapeDtypeStruct((peers_y, piece_rows, LANES), bf16),
             scratch_shapes=[
-                pltpu.VMEM((peers * slots + 1, B, LANES), bf16),
+                pltpu.VMEM((peers * slots + 1, HALF, LANES), bf16),
                 pltpu.VMEM((sums + 1, HALF, LANES), jnp.float32),
                 pltpu.VMEM((sums + 1, HALF, LANES), jnp.float32),
                 pltpu.VMEM((RING, CHUNK, B, LANES), bf16),
+                pltpu.VMEM((peers_y, piece_rows, LANES), bf16),
                 pltpu.SMEM((coarse_here,), jnp.int32),
                 pltpu.SMEM((peers_y * CCAP,), jnp.int32),
                 pltpu.SMEM((peers_y,), jnp.int32),
                 pltpu.SemaphoreType.DMA,
+                pltpu.SemaphoreType.DMA,
+                pltpu.SemaphoreType.DMA,
                 pltpu.SemaphoreType.DMA((RING,)),
+                pltpu.SemaphoreType.DMA((coarse_here,)),
             ],
             compiler_params=pltpu.CompilerParams(vmem_limit_bytes=56 * MIB),
             cost_estimate=pl.CostEstimate(flops=4_000_000_000, bytes_accessed=8_000_000, transcendentals=0),
         )(meta, count, coarse_target, arrived, local, tiles)
         received.append(lax.all_to_all(sent, "py", split_axis=0, concat_axis=0, tiled=True))
 
-    per_step = 3
+    per_step = 9
     out_groups = coarse_here // GROUP
     placed = None
     for part in range(PIECES):
@@ -544,7 +577,7 @@
             in_specs=[whole((peers_y, piece_rows, LANES))] + ([hbm] if part else []),
             out_specs=pl.BlockSpec((per_step, out_groups, KROWS, LANES), lambda s, first=first: (first + s, 0, 0, 0)),
             out_shape=jax.ShapeDtypeStruct((S, out_groups, KROWS, LANES), bf16),
-            scratch_shapes=[pltpu.SMEM((coarse_here,), jnp.int32), pltpu.SMEM((coarse_here,), jnp.int32)],
+            scratch_shapes=[pltpu.SMEM((coarse_here + 1,), jnp.int32), pltpu.SMEM((coarse_here + 1,), jnp.int32)],
             input_output_aliases={1: 0} if part else {},
             compiler_params=pltpu.CompilerParams(vmem_limit_bytes=24 * MIB),
             cost_estimate=pl.CostEstimate(flops=1_000_000_000, bytes_accessed=3_000_000, transcendentals=0),

time: 131 us -> 127 us (0.969)
  Pallas kernels: 71.8 us -> 69.8 us
  local copies, waits for them, and re-layouts: 1.32 us -> 0 us
    pallas_call x1, Pallas kernels: 5.81 us -> 3.41 us  [body(): pl.pallas_call(place_kernel, grid=(PS // per_step,), in_specs=[whole((pee...]
    unnamed x2 -> x0, local copies, waits for them, and re-layouts: 1.32 us -> none
  transfers between devices with their start and end apart: 1 -> 1, of which waited for: 1 -> 1; matrix products, arithmetic and copies ran while one was open for 0% -> 0% of each run, Pallas kernels for 35% -> 36%
where the time goes in v4:
time: 127 us; the launch traced here: 126 us
  Pallas kernels  69.8 us (55%)
  blocking collectives  46 us (36%)
  starting transfers between devices  7.43 us (6%)
  waiting for transfers between devices  3.16 us (2%)
    all_to_all x1, blocking collectives, body(): lax.all_to_all(sent, 'py', split_axis=0, concat_axis=0, tiled=True)  46 us
    pallas_call x1, Pallas kernels, body(): pl.pallas_call(functools.partial(project_kernel, peers * slots), grid=(gr...  45.7 us
    pallas_call x1, Pallas kernels, body(): pl.pallas_call(functools.partial(combine_kernel, part), in_specs=[smem, s...  16.3 us
    all_to_all x1, starting transfers between devices, body(): lax.all_to_all(outgoing.reshape(peers, slots, HALF, LANES), ('px', 'py'),...  7.43 us
    pallas_call x1, Pallas kernels, body(): pl.pallas_call(pack_kernel, in_specs=[hbm, hbm], out_specs=[hbm, hbm], ou...  4.31 us
    pallas_call x1, Pallas kernels, body(): pl.pallas_call(place_kernel, grid=(PS // per_step,), in_specs=[whole((pee...  3.41 us
    all_to_all x1, waiting for transfers between devices, body(): lax.all_to_all(outgoing.reshape(peers, slots, HALF, LANES), ('px', 'py'),...  3.16 us
  transfers between devices with their start and end apart: 1, of which 1 were waited for; matrix products, arithmetic and copies ran while one was open for 0% of the time, Pallas kernels for 36%

profile of v4, /device:TPU:0, one launch (start us, length us, event | category | flops | bytes accessed | tf_op | source)
XLA Modules:
  0.0 126.4 jit_solution(17845271052770874213)
XLA Ops:
  0.0 4.3 %shard_map.73 = (bf16[256,32,128]{2,1,0:T(8,128)(2,1)}, bf16[96,32,128]{2,1,0:T(8,128)(2,1)}) custom-call(s32[8,32]{1,0:T(8,128)} %bitcast.30, bf16[12,256,128]{2,1,0:T(8,128)(2,1)} %bitcast.28), custom_call_target="tpu_custom_call" | custom-call | tf_op jit(solution)/shard_map/pallas_call | solution.py:475
  4.3 7.4 %all-to-all-start = ((bf16[32,8,32,128]{3,2,1,0:T(8,128)(2,1)}), bf16[32,8,32,128]{3,2,1,0:T(8,128)(2,1)}, u32[]{:S(2)}, u32[]{:S(2)}) async-start(bf16[32,8,32,128]{3,2,1,0:T(8,128)(2,1)} %bitcast.27), calls=%async_computation | async-start | bytes 4194304 | tf_op jit(solution)/shard_map/all_to_all | solution.py:495
  11.8 45.7 %shard_map.74 = (f32[432,32,128]{2,1,0:T(8,128)}, bf16[1,1728,64,128]{3,2,1,0:T(8,128)(2,1)}, s32[2,1728]{1,0:T(2,128)}, s32[1]{0:T(128)}) custom-call(s32[27,96]{1,0:T(8,128)} %bitcast.32, s32[27,96]{1,0:T(8,128)} %bitcast.33, s32[1,96]{1,0:T(1,128)} %bitcast.34, bf16[27,12,256,128]{3,2,1,0:T(8,128)(2,1)} %bitcast.31, bf16[12,256,128]{2,1,0:T(8,128)(2,1)} %bitcast.29, ...), custom_call_target="tpu_custom_call" | custom-call | flops 22548578304 | bytes 45000000 | tf_op jit(solution)/shard_map/pallas_call | solution.py:501
  57.5 3.2 %all-to-all-done = bf16[32,8,32,128]{3,2,1,0:T(8,128)(2,1)} async-done(((bf16[32,8,32,128]{3,2,1,0:T(8,128)(2,1)}), bf16[32,8,32,128]{3,2,1,0:T(8,128)(2,1)}, u32[]{:S(2)}, u32[]{:S(2)}) %all-to-all-start) | async-done | bytes 2097184 | tf_op jit(solution)/shard_map/all_to_all | solution.py:495
  60.6 16.3 %shard_map.75 = bf16[8,1744,128]{2,1,0:T(8,128)(2,1)} custom-call(s32[2,1728]{1,0:T(2,128)} %get-tuple-element.12.meta_ref, s32[1]{0:T(128)} %get-tuple-element.13.count_ref, s32[16]{0:T(128)} %target_ref.1, bf16[256,32,128]{2,1,0:T(8,128)(2,1)} %bitcast.15.ghost_hbm, f32[432,32,128]{2,1,0:T(8,128)} %get-tuple-element.15.sum_hbm, ...), custom_call_target="tpu_custom_call" | custom-call | flops 4000000000 | bytes 8000000 | tf_op jit(solution)/shard_map/pallas_call | solution.py:544
  77.0 46.0 %all_to_all.10.in_ref = bf16[8,1744,128]{2,1,0:T(8,128)(2,1)S(1)} all-to-all(bf16[8,1744,128]{2,1,0:T(8,128)(2,1)} %shard_map.75), channel_id=1, replica_groups=mesh['px'=4,'py'=8] {'py'}, dimensions={0} | all-to-all | bytes 7143424 | tf_op jit(solution)/shard_map/all_to_all | solution.py:567
  123.0 3.4 %shard_map.76 = bf16[27,2,256,128]{3,2,1,0:T(8,128)(2,1)} custom-call(bf16[8,1744,128]{2,1,0:T(8,128)(2,1)S(1)} %all_to_all.10.in_ref), custom_call_target="tpu_custom_call" | custom-call | flops 1000000000 | bytes 3000000 | tf_op jit(solution)/shard_map/pallas_call | solution.py:574
Async XLA Ops:
  4.3 56.3 %all-to-all-start = ((bf16[32,8,32,128]{3,2,1,0:T(8,128)(2,1)}), bf16[32,8,32,128]{3,2,1,0:T(8,128)(2,1)}, u32[]{:S(2)}, u32[]{:S(2)}) async-start(bf16[32,8,32,128]{3,2,1,0:T(8,128)(2,1)} %bitcast.27), calls=%async_computation | async-start | bytes 4194304 | tf_op jit(solution)/shard_map/all_to_all | solution.py:495

commit v5 on v4

--- a/solution.py
+++ b/solution.py
@@ -195,10 +195,9 @@
         for r in range(GROUP):
             row = step * GROUP + r
             moving = both[r * B : (r + 1) * B]
-            weights, targets = [], []
             for h in range(2):
                 tile = moving[:, h * LANES : (h + 1) * LANES]
-                halves = []
+                halves, targets = [], []
                 for parity, table, listed in ((0, first_ref, even_tiles), (1, second_ref, odd_tiles)):
                     k = 2 * (pair + h) + parity
                     if k >= per_row:
@@ -215,14 +214,11 @@
                         here_ref[parity, at] = note
                         counts[parity] = at + (note >> FLAG_BIT)
                 filled = jnp.concatenate(halves, axis=0)
-                blank = jnp.zeros_like(filled)
-                weights.append(jnp.concatenate([filled, blank] if h == 0 else [blank, filled], axis=1))
-            value = jnp.dot(moving, jnp.concatenate(weights, axis=0), preferred_element_type=jnp.float32)
-            for h in range(2):
-                even, odd = fold(value[:, h * LANES : (h + 1) * LANES], low_half)
-                sum_ref[targets[2 * h]] += even
-                if targets[2 * h + 1] is not None:
-                    odd_ref[targets[2 * h + 1]] += odd
+                value = jnp.dot(tile, filled, preferred_element_type=jnp.float32)
+                even, odd = fold(value, low_half)
+                sum_ref[targets[0]] += even
+                if targets[1] is not None:
+                    odd_ref[targets[1]] += odd
 
     no_entry = (ghosts << PLACE_BITS) + sums
     for part in range(PIECES):
@@ -290,14 +286,17 @@
 
 
 def combine_kernel(
-    part, meta_ref, count_ref, target_ref, ghost_hbm, sum_hbm, tiles_hbm, out_hbm,
-    ghost_ref, even_ref, odd_ref, tiles_ref, out_ref, bucket_ref, place_ref, per_peer_ref,
-    ghost_sem, sum_sem, note_sem, sems, out_sems,
+    part, peers, meta_ref, count_ref, target_ref, me_ref, ghost_hbm, sum_hbm, tiles_hbm, *rest
 ):
+    outs = rest[:peers]
+    (
+        ghost_ref, even_ref, odd_ref, tiles_ref, out_ref, bucket_ref, place_ref, per_peer_ref,
+        ghost_sem, sum_sem, note_sems, sems, out_sems,
+    ) = rest[peers:]
+    me = me_ref[0]
     ghosts = ghost_hbm.shape[0]
     coarse_here = target_ref.shape[0]
     sums = coarse_here * PS
-    peers = out_ref.shape[0]
     chunks = count_ref[part]
     low_half = lane_low(HALF)
     zero_half = jnp.zeros((HALF, LANES), jnp.bfloat16)
@@ -345,14 +344,18 @@
     def note(p, carry):
         value = jnp.full(second_slot.shape, -1, jnp.int32)
         for q in range(CCAP):
-            value = jnp.where(second_slot == q, place_ref[p * CCAP + q], value)
+            value = jnp.where(second_slot == q, place_ref[(p ^ me) * CCAP + q], value)
         out_ref[p, payload:] = value.astype(jnp.float32).astype(jnp.bfloat16)
         return carry
 
     lax.fori_loop(0, peers, note, 0)
     notes = pl.ds(payload, out_ref.shape[1] - payload)
-    put_notes = pltpu.make_async_copy(out_ref.at[:, notes], out_hbm.at[:, notes], note_sem)
-    put_notes.start()
+
+    def put_notes(d):
+        return pltpu.make_async_copy(out_ref.at[d, notes], outs[d].at[notes], note_sems.at[d])
+
+    for d in range(peers):
+        put_notes(d).start()
     load_ghosts.wait()
     load_sums.wait()
 
@@ -363,68 +366,68 @@
 
         fetch(i).wait()
         slot = lax.rem(i, RING)
-        for j in range(0, CHUNK, 2):
-            weights, targets = [], []
-            for h in range(2):
-                at = i * CHUNK + j + h
-                even, odd = meta_ref[2 * part, at], meta_ref[2 * part + 1, at]
-                first = ghost_ref[(even >> PLACE_BITS) & ((1 << FLAG_BIT - PLACE_BITS) - 1)]
-                second = ghost_ref[(odd >> PLACE_BITS) & ((1 << FLAG_BIT - PLACE_BITS) - 1)]
-                targets += [even & ((1 << PLACE_BITS) - 1), odd & ((1 << PLACE_BITS) - 1)]
-                filled = jnp.concatenate(
-                    [
-                        jnp.where(low_half, first, zero_half),
-                        jnp.where(low_half, swap_halves(first), zero_half),
-                        jnp.where(low_half, zero_half, swap_halves(second)),
-                        jnp.where(low_half, zero_half, second),
-                    ],
-                    axis=0,
-                )
-                blank = jnp.zeros_like(filled)
-                weights.append(jnp.concatenate([filled, blank] if h == 0 else [blank, filled], axis=1))
-            moving = jnp.concatenate([tiles_ref[slot, j], tiles_ref[slot, j + 1]], axis=1)
-            value = jnp.dot(moving, jnp.concatenate(weights, axis=0), preferred_element_type=jnp.float32)
-            for h in range(2):
-                even, odd = fold(value[:, h * LANES : (h + 1) * LANES], low_half)
-                even_ref[targets[2 * h]] += even
-                odd_ref[targets[2 * h + 1]] += odd
+        for j in range(CHUNK):
+            at = i * CHUNK + j
+            even, odd = meta_ref[2 * part, at], meta_ref[2 * part + 1, at]
+            first = ghost_ref[(even >> PLACE_BITS) & ((1 << FLAG_BIT - PLACE_BITS) - 1)]
+            second = ghost_ref[(odd >> PLACE_BITS) & ((1 << FLAG_BIT - PLACE_BITS) - 1)]
+            filled = jnp.concatenate(
+                [
+                    jnp.where(low_half, first, zero_half),
+                    jnp.where(low_half, swap_halves(first), zero_half),
+                    jnp.where(low_half, zero_half, swap_halves(second)),
+                    jnp.where(low_half, zero_half, second),
+                ],
+                axis=0,
+            )
+            value = jnp.dot(tiles_ref[slot, j], filled, preferred_element_type=jnp.float32)
+            to_even, to_odd = fold(value, low_half)
+            even_ref[even & ((1 << PLACE_BITS) - 1)] += to_even
+            odd_ref[odd & ((1 << PLACE_BITS) - 1)] += to_odd
         return carry
 
     lax.fori_loop(0, chunks, work, 0)
 
-    def put(c):
-        bucket = bucket_ref[c]
-        span = pl.ds(pl.multiple_of(lax.rem(bucket, CCAP) * (PS * HALF), HALF), PS * HALF)
-        peer = lax.div(bucket, CCAP)
-        return pltpu.make_async_copy(out_ref.at[peer, span], out_hbm.at[peer, span], out_sems.at[c])
+    def put(c, d, start):
+        span = pl.ds(start, PS * HALF)
+        return pltpu.make_async_copy(out_ref.at[d, span], outs[d].at[span], out_sems.at[c])
 
     def finish(c, carry):
         bucket = bucket_ref[c]
-        start = lax.rem(bucket, CCAP) * (PS * HALF)
-        peer = lax.div(bucket, CCAP)
+        start = pl.multiple_of(lax.rem(bucket, CCAP) * (PS * HALF), HALF)
+        offset = lax.div(bucket, CCAP) ^ me
         first = c * PS
         for s in range(PS):
             total = even_ref[first + s] + odd_ref[first + s]
-            here = pl.multiple_of(start + s * HALF, HALF)
-            out_ref[peer, pl.ds(here, HALF)] = total.astype(jnp.bfloat16)
-        put(c).start()
+            out_ref[offset, pl.ds(pl.multiple_of(start + s * HALF, HALF), HALF)] = total.astype(jnp.bfloat16)
+        for d in range(peers):
+
+            @pl.when(offset == d)
+            def _():
+                put(c, d, start).start()
+
         return carry
 
     lax.fori_loop(0, coarse_here, finish, 0)
-    put_notes.wait()
-    lax.fori_loop(0, coarse_here, lambda c, carry: (put(c).wait(), carry)[1], 0)
-
-
-def place_kernel(in_ref, *rest):
-    out_ref, peer_ref, start_ref = rest[-3:]
+    for d in range(peers):
+        put_notes(d).wait()
+    lax.fori_loop(0, coarse_here, lambda c, carry: (put(c, 0, 0).wait(), carry)[1], 0)
+
+
+def place_kernel(peers, *refs):
+    parts = refs[:peers]
+    out_ref, in_ref, peer_ref, start_ref, sems = refs[peers:]
     step = pl.program_id(0)
-    peers = in_ref.shape[0]
     per_step, groups = out_ref.shape[0], out_ref.shape[1]
     payload = CCAP * PS * HALF
 
     @pl.when(step == 0)
     def _():
+        loads = [pltpu.make_async_copy(parts[d], in_ref.at[d], sems.at[d]) for d in range(peers)]
+        for load in loads:
+            load.start()
         for p in range(peers):
+            loads[p].wait()
             notes = in_ref[p, payload:].astype(jnp.float32)
             which = lax.broadcasted_iota(jnp.int32, notes.shape, 1) // HALF
             for q in range(CCAP):
@@ -539,49 +542,51 @@
     )(a_source.T, coarse_slot.T, agg_local.reshape(1, rows), a_tiles, p_tiles, own)
 
     piece_rows = CCAP * PS * HALF + 16
-    received = []
-    for part in range(PIECES):
-        sent = pl.pallas_call(
-            functools.partial(combine_kernel, part),
-            in_specs=[smem, smem, smem, hbm, hbm, hbm],
-            out_specs=hbm,
-            out_shape=jax.ShapeDtypeStruct((peers_y, piece_rows, LANES), bf16),
-            scratch_shapes=[
-                pltpu.VMEM((peers * slots + 1, HALF, LANES), bf16),
-                pltpu.VMEM((sums + 1, HALF, LANES), jnp.float32),
-                pltpu.VMEM((sums + 1, HALF, LANES), jnp.float32),
-                pltpu.VMEM((RING, CHUNK, B, LANES), bf16),
-                pltpu.VMEM((peers_y, piece_rows, LANES), bf16),
-                pltpu.SMEM((coarse_here,), jnp.int32),
-                pltpu.SMEM((peers_y * CCAP,), jnp.int32),
-                pltpu.SMEM((peers_y,), jnp.int32),
-                pltpu.SemaphoreType.DMA,
-                pltpu.SemaphoreType.DMA,
-                pltpu.SemaphoreType.DMA,
-                pltpu.SemaphoreType.DMA((RING,)),
-                pltpu.SemaphoreType.DMA((coarse_here,)),
-            ],
-            compiler_params=pltpu.CompilerParams(vmem_limit_bytes=56 * MIB),
-            cost_estimate=pl.CostEstimate(flops=4_000_000_000, bytes_accessed=8_000_000, transcendentals=0),
-        )(meta, count, coarse_target, arrived, local, tiles)
-        received.append(lax.all_to_all(sent, "py", split_axis=0, concat_axis=0, tiled=True))
+    me = lax.axis_index("py").reshape(1)
+    sent = pl.pallas_call(
+        functools.partial(combine_kernel, 0, peers_y),
+        in_specs=[smem, smem, smem, smem, hbm, hbm, hbm],
+        out_specs=[hbm] * peers_y,
+        out_shape=[jax.ShapeDtypeStruct((piece_rows, LANES), bf16)] * peers_y,
+        scratch_shapes=[
+            pltpu.VMEM((peers * slots + 1, HALF, LANES), bf16),
+            pltpu.VMEM((sums + 1, HALF, LANES), jnp.float32),
+            pltpu.VMEM((sums + 1, HALF, LANES), jnp.float32),
+            pltpu.VMEM((RING, CHUNK, B, LANES), bf16),
+            pltpu.VMEM((peers_y, piece_rows, LANES), bf16),
+            pltpu.SMEM((coarse_here,), jnp.int32),
+            pltpu.SMEM((peers_y * CCAP,), jnp.int32),
+            pltpu.SMEM((peers_y,), jnp.int32),
+            pltpu.SemaphoreType.DMA,
+            pltpu.SemaphoreType.DMA,
+            pltpu.SemaphoreType.DMA((peers_y,)),
+            pltpu.SemaphoreType.DMA((RING,)),
+            pltpu.SemaphoreType.DMA((coarse_here,)),
+        ],
+        compiler_params=pltpu.CompilerParams(vmem_limit_bytes=56 * MIB),
+        cost_estimate=pl.CostEstimate(flops=4_000_000_000, bytes_accessed=8_000_000, transcendentals=0),
+    )(meta, count, coarse_target, me, arrived, local, tiles)
+    received = [sent[0]]
+    for d in range(1, peers_y):
+        received.append(lax.ppermute(sent[d], "py", [(i, i ^ d) for i in range(peers_y)]))
 
     per_step = 9
     out_groups = coarse_here // GROUP
-    placed = None
-    for part in range(PIECES):
-        first = part * PS // per_step
-        placed = pl.pallas_call(
-            place_kernel,
-            grid=(PS // per_step,),
-            in_specs=[whole((peers_y, piece_rows, LANES))] + ([hbm] if part else []),
-            out_specs=pl.BlockSpec((per_step, out_groups, KROWS, LANES), lambda s, first=first: (first + s, 0, 0, 0)),
-            out_shape=jax.ShapeDtypeStruct((S, out_groups, KROWS, LANES), bf16),
-            scratch_shapes=[pltpu.SMEM((coarse_here + 1,), jnp.int32), pltpu.SMEM((coarse_here + 1,), jnp.int32)],
-            input_output_aliases={1: 0} if part else {},
-            compiler_params=pltpu.CompilerParams(vmem_limit_bytes=24 * MIB),
-            cost_estimate=pl.CostEstimate(flops=1_000_000_000, bytes_accessed=3_000_000, transcendentals=0),
-        )(received[part], *([placed] if part else []))
+    placed = pl.pallas_call(
+        functools.partial(place_kernel, peers_y),
+        grid=(S // per_step,),
+        in_specs=[hbm] * peers_y,
+        out_specs=pl.BlockSpec((per_step, out_groups, KROWS, LANES), lambda s: (s, 0, 0, 0)),
+        out_shape=jax.ShapeDtypeStruct((S, out_groups, KROWS, LANES), bf16),
+        scratch_shapes=[
+            pltpu.VMEM((peers_y, piece_rows, LANES), bf16),
+            pltpu.SMEM((coarse_here + 1,), jnp.int32),
+            pltpu.SMEM((coarse_here + 1,), jnp.int32),
+            pltpu.SemaphoreType.DMA((peers_y,)),
+        ],
+        compiler_params=pltpu.CompilerParams(vmem_limit_bytes=24 * MIB),
+        cost_estimate=pl.CostEstimate(flops=1_000_000_000, bytes_accessed=3_000_000, transcendentals=0),
+    )(*received)
     return from_tiles(placed).transpose(1, 0, 2)
 
 

time: 127 us -> 127 us (level)
  blocking collectives: 46 us -> 0 us
  waiting for transfers between devices: 3.16 us -> 42.5 us
  starting transfers between devices: 7.43 us -> 14.2 us
    all_to_all x1 -> x0, blocking collectives: 46 us -> none  [body(): lax.all_to_all(sent, 'py', split_axis=0, concat_axis=0, tiled=True)]
    ppermute x0 -> x7, waiting for transfers between devices: none -> 36 us  [body(): lax.ppermute(sent[d], 'py', [(i, i ^ d) for i in range(peers_y)])]
    ppermute x0 -> x7, starting transfers between devices: none -> 6.78 us  [body(): lax.ppermute(sent[d], 'py', [(i, i ^ d) for i in range(peers_y)])]
    pallas_call x1, Pallas kernels: 45.7 us -> 42.4 us  [body(): pl.pallas_call(functools.partial(project_kernel, peers * slots), grid=(gr...]
    all_to_all x1, waiting for transfers between devices: 3.16 us -> 6.48 us  [body(): lax.all_to_all(outgoing.reshape(peers, slots, HALF, LANES), ('px', 'py'),...]
    pallas_call x2, Pallas kernels: 19.7 us -> 22.2 us  [the longest x1 15.5 us: body(): pl.pallas_call(functools.partial(combine_kernel, 0, peers_y), in_specs=[s...]
  transfers between devices with their start and end apart: 1 -> 8, of which waited for: 1 -> 4; matrix products, arithmetic and copies ran while one was open for 0% -> 0% of each run, Pallas kernels for 36% -> 33%
where the time goes in v5:
time: 127 us
  Pallas kernels  68.9 us (54%)
  waiting for transfers between devices  42.5 us (33%)
  starting transfers between devices  14.2 us (11%)
    pallas_call x1, Pallas kernels, body(): pl.pallas_call(functools.partial(project_kernel, peers * slots), grid=(gr...  42.4 us
    ppermute x7, waiting for transfers between devices, body(): lax.ppermute(sent[d], 'py', [(i, i ^ d) for i in range(peers_y)])  36 us
    pallas_call x1, Pallas kernels, body(): pl.pallas_call(functools.partial(combine_kernel, 0, peers_y), in_specs=[s...  15.5 us
    all_to_all x1, starting transfers between devices, body(): lax.all_to_all(outgoing.reshape(peers, slots, HALF, LANES), ('px', 'py'),...  7.43 us
    ppermute x7, starting transfers between devices, body(): lax.ppermute(sent[d], 'py', [(i, i ^ d) for i in range(peers_y)])  6.78 us
    pallas_call x1, Pallas kernels, body(): pl.pallas_call(functools.partial(place_kernel, peers_y), grid=(S // per_s...  6.73 us
    all_to_all x1, waiting for transfers between devices, body(): lax.all_to_all(outgoing.reshape(peers, slots, HALF, LANES), ('px', 'py'),...  6.48 us
    pallas_call x1, Pallas kernels, body(): pl.pallas_call(pack_kernel, in_specs=[hbm, hbm], out_specs=[hbm, hbm], ou...  4.31 us
  transfers between devices with their start and end apart: 8, of which 4 were waited for; matrix products, arithmetic and copies ran while one was open for 0% of the time, Pallas kernels for 33%

profile of v5, /device:TPU:0, one launch (start us, length us, event | category | flops | bytes accessed | tf_op | source)
XLA Modules:
  0.0 126.6 jit_solution(1926803606569686931)
XLA Ops:
  0.0 4.3 %shard_map.73 = (bf16[256,32,128]{2,1,0:T(8,128)(2,1)}, bf16[96,32,128]{2,1,0:T(8,128)(2,1)}) custom-call(s32[8,32]{1,0:T(8,128)} %bitcast.31, bf16[12,256,128]{2,1,0:T(8,128)(2,1)} %bitcast.29), custom_call_target="tpu_custom_call" | custom-call | tf_op jit(solution)/shard_map/pallas_call | solution.py:478
  4.3 7.4 %all-to-all-start = ((bf16[32,8,32,128]{3,2,1,0:T(8,128)(2,1)}), bf16[32,8,32,128]{3,2,1,0:T(8,128)(2,1)}, u32[]{:S(2)}, u32[]{:S(2)}) async-start(bf16[32,8,32,128]{3,2,1,0:T(8,128)(2,1)} %bitcast.28), calls=%async_computation | async-start | bytes 4194304 | tf_op jit(solution)/shard_map/all_to_all | solution.py:498
  11.8 42.4 %shard_map.74 = (f32[432,32,128]{2,1,0:T(8,128)}, bf16[1,1728,64,128]{3,2,1,0:T(8,128)(2,1)}, s32[2,1728]{1,0:T(2,128)}, s32[1]{0:T(128)}) custom-call(s32[27,96]{1,0:T(8,128)} %bitcast.33, s32[27,96]{1,0:T(8,128)} %bitcast.34, s32[1,96]{1,0:T(1,128)} %bitcast.35, bf16[27,12,256,128]{3,2,1,0:T(8,128)(2,1)} %bitcast.32, bf16[12,256,128]{2,1,0:T(8,128)(2,1)} %bitcast.30, ...), custom_call_target="tpu_custom_call" | custom-call | flops 22548578304 | bytes 45000000 | tf_op jit(solution)/shard_map/pallas_call | solution.py:504
  54.1 6.5 %all-to-all-done = bf16[32,8,32,128]{3,2,1,0:T(8,128)(2,1)} async-done(((bf16[32,8,32,128]{3,2,1,0:T(8,128)(2,1)}), bf16[32,8,32,128]{3,2,1,0:T(8,128)(2,1)}, u32[]{:S(2)}, u32[]{:S(2)}) %all-to-all-start) | async-done | bytes 2097184 | tf_op jit(solution)/shard_map/all_to_all | solution.py:498
  60.6 15.5 %shard_map.75 = (bf16[1744,128]{1,0:T(8,128)(2,1)}, bf16[1744,128]{1,0:T(8,128)(2,1)}, bf16[1744,128]{1,0:T(8,128)(2,1)}, bf16[1744,128]{1,0:T(8,128)(2,1)}, bf1...) custom-call(s32[2,1728]{1,0:T(2,128)} %get-tuple-element.20.meta_ref,, ...), custom_call_target="tpu_custom_call" | custom-call | flops 4000000000 | bytes 8000000 | tf_op jit(solution)/shard_map/pallas_call | solution.py:546
  76.1 0.1 collective-permute-start
  76.2 1.0 collective-permute-start.1
  77.2 0.8 collective-permute-start.2
  78.0 1.3 collective-permute-start.3
  79.3 0.4 collective-permute-start.4
  79.7 0.0 collective-permute-done.refs_1_
  79.7 2.2 %collective-permute-start.5 = (bf16[1744,128]{1,0:T(8,128)(2,1)}, bf16[1744,128]{1,0:T(8,128)(2,1)S(1)}, u32[]{:S(2)}, u32[]{:S(2)}) collective-permute-start(bf16[1744,128]{1,0:T(8,128)(2,1)} %get-tuple-element.31), channel_id=1, source_target_pairs={{0,6},{1,7},{2,4},{3,5},{4,2},{5,3},{6,0},{7,1},{8,14},{9,15},{10,... | collective-permute-start | bytes 1339400 | tf_op jit(solution)/shard_map/ppermute | solution.py:571
  81.9 7.6 %collective-permute-done.1.refs_2_ = bf16[1744,128]{1,0:T(8,128)(2,1)S(1)} collective-permute-done((bf16[1744,128]{1,0:T(8,128)(2,1)}, bf16[1744,128]{1,0:T(8,128)(2,1)S(1)}, u32[]{:S(2)}, u32[]{:S(2)}) %collective-permute-start.1) | collective-permute-done | bytes 446496 | tf_op jit(solution)/shard_map/ppermute | solution.py:571
  89.5 1.0 collective-permute-start.6
  90.5 7.7 %collective-permute-done.2.refs_3_ = bf16[1744,128]{1,0:T(8,128)(2,1)S(1)} collective-permute-done((bf16[1744,128]{1,0:T(8,128)(2,1)}, bf16[1744,128]{1,0:T(8,128)(2,1)S(1)}, u32[]{:S(2)}, u32[]{:S(2)}) %collective-permute-start.2) | collective-permute-done | bytes 446496 | tf_op jit(solution)/shard_map/ppermute | solution.py:571
  98.2 0.0 collective-permute-done.3.refs_4_
  98.2 20.7 %collective-permute-done.4.refs_5_ = bf16[1744,128]{1,0:T(8,128)(2,1)S(1)} collective-permute-done((bf16[1744,128]{1,0:T(8,128)(2,1)}, bf16[1744,128]{1,0:T(8,128)(2,1)S(1)}, u32[]{:S(2)}, u32[]{:S(2)}) %collective-permute-start.4) | collective-permute-done | bytes 446496 | tf_op jit(solution)/shard_map/ppermute | solution.py:571
  118.9 0.0 collective-permute-done.5.refs_6_
  118.9 0.0 collective-permute-done.6.refs_7_
  118.9 0.0 copy-start
  118.9 1.0 copy-done
  119.9 6.7 %shard_map.76 = bf16[27,2,256,128]{3,2,1,0:T(8,128)(2,1)} custom-call(bf16[1744,128]{1,0:T(8,128)(2,1)S(1)} %copy-done, bf16[1744,128]{1,0:T(8,128)(2,1)S(1)} %collective-permute-done.refs_1_, bf16[1744,128]{1,0:T(8,128)(2,1)S(1)} %collective-permute-done.1.refs_2_, bf16[1744,128]{1,0:T(8,128)(2,1)S(1)} %collective-permute-done.2.refs_3_, ...), custom_call_target="tpu_custom_call" | custom-call | flops 1000000000 | bytes 3000000 | tf_op jit(solution)/shard_map/pallas_call | solution.py:575
Async XLA Ops:
  4.3 56.3 %all-to-all-start = ((bf16[32,8,32,128]{3,2,1,0:T(8,128)(2,1)}), bf16[32,8,32,128]{3,2,1,0:T(8,128)(2,1)}, u32[]{:S(2)}, u32[]{:S(2)}) async-start(bf16[32,8,32,128]{3,2,1,0:T(8,128)(2,1)} %bitcast.28), calls=%async_computation | async-start | bytes 4194304 | tf_op jit(solution)/shard_map/all_to_all | solution.py:498
  76.1 3.6 %collective-permute-start = (bf16[1744,128]{1,0:T(8,128)(2,1)}, bf16[1744,128]{1,0:T(8,128)(2,1)S(1)}, u32[]{:S(2)}, u32[]{:S(2)}) collective-permute-start(bf16[1744,128]{1,0:T(8,128)(2,1)} %get-tuple-element.26), channel_id=1, source_target_pairs={{0,1},{1,0},{2,3},{3,2},{4,5},{5,4},{6,7},{7,6},{8,9},{9,8},{10,11... | collective-permute-start | bytes 1339400 | tf_op jit(solution)/shard_map/ppermute | solution.py:571
  76.2 13.3 %collective-permute-start.1 = (bf16[1744,128]{1,0:T(8,128)(2,1)}, bf16[1744,128]{1,0:T(8,128)(2,1)S(1)}, u32[]{:S(2)}, u32[]{:S(2)}) collective-permute-start(bf16[1744,128]{1,0:T(8,128)(2,1)} %get-tuple-element.27), channel_id=1, source_target_pairs={{0,2},{1,3},{2,0},{3,1},{4,6},{5,7},{6,4},{7,5},{8,10},{9,11},{10,... | collective-permute-start | bytes 1339400 | tf_op jit(solution)/shard_map/ppermute | solution.py:571
  77.2 21.0 %collective-permute-start.2 = (bf16[1744,128]{1,0:T(8,128)(2,1)}, bf16[1744,128]{1,0:T(8,128)(2,1)S(1)}, u32[]{:S(2)}, u32[]{:S(2)}) collective-permute-start(bf16[1744,128]{1,0:T(8,128)(2,1)} %get-tuple-element.28), channel_id=1, source_target_pairs={{0,3},{1,2},{2,1},{3,0},{4,7},{5,6},{6,5},{7,4},{8,11},{9,10},{10,... | collective-permute-start | bytes 1339400 | tf_op jit(solution)/shard_map/ppermute | solution.py:571
  78.0 20.1 %collective-permute-start.3 = (bf16[1744,128]{1,0:T(8,128)(2,1)}, bf16[1744,128]{1,0:T(8,128)(2,1)S(1)}, u32[]{:S(2)}, u32[]{:S(2)}) collective-permute-start(bf16[1744,128]{1,0:T(8,128)(2,1)} %get-tuple-element.29), channel_id=1, source_target_pairs={{0,4},{1,5},{2,6},{3,7},{4,0},{5,1},{6,2},{7,3},{8,12},{9,13},{10,... | collective-permute-start | bytes 1339400 | tf_op jit(solution)/shard_map/ppermute | solution.py:571
  79.3 39.6 %collective-permute-start.4 = (bf16[1744,128]{1,0:T(8,128)(2,1)}, bf16[1744,128]{1,0:T(8,128)(2,1)S(1)}, u32[]{:S(2)}, u32[]{:S(2)}) collective-permute-start(bf16[1744,128]{1,0:T(8,128)(2,1)} %get-tuple-element.30), channel_id=1, source_target_pairs={{0,5},{1,4},{2,7},{3,6},{4,1},{5,0},{6,3},{7,2},{8,13},{9,12},{10,... | collective-permute-start | bytes 1339400 | tf_op jit(solution)/shard_map/ppermute | solution.py:571
  79.7 39.1 %collective-permute-start.5 = (bf16[1744,128]{1,0:T(8,128)(2,1)}, bf16[1744,128]{1,0:T(8,128)(2,1)S(1)}, u32[]{:S(2)}, u32[]{:S(2)}) collective-permute-start(bf16[1744,128]{1,0:T(8,128)(2,1)} %get-tuple-element.31), channel_id=1, source_target_pairs={{0,6},{1,7},{2,4},{3,5},{4,2},{5,3},{6,0},{7,1},{8,14},{9,15},{10,... | collective-permute-start | bytes 1339400 | tf_op jit(solution)/shard_map/ppermute | solution.py:571
  89.5 29.4 %collective-permute-start.6 = (bf16[1744,128]{1,0:T(8,128)(2,1)}, bf16[1744,128]{1,0:T(8,128)(2,1)S(1)}, u32[]{:S(2)}, u32[]{:S(2)}) collective-permute-start(bf16[1744,128]{1,0:T(8,128)(2,1)} %get-tuple-element.32), channel_id=1, source_target_pairs={{0,7},{1,6},{2,5},{3,4},{4,3},{5,2},{6,1},{7,0},{8,15},{9,14},{10,... | collective-permute-start | bytes 1339400 | tf_op jit(solution)/shard_map/ppermute | solution.py:571
  118.9 1.0 copy-start

commit v6 on v5

--- a/solution.py
+++ b/solution.py
@@ -17,8 +17,7 @@
 GROUP = 8
 TILES = FLAT // LANES
 KROWS = GROUP * TILES
-PIECES = 1
-PS = S // PIECES
+PIECES = 2
 CHUNK = 32
 PEERS = 8
 TURN = 8
@@ -121,7 +120,7 @@
 
 
 def project_kernel(
-    ghosts, source_ref, slot_ref, agg_ref, a_ref, p_ref, own_ref, sum_ref, tiles_hbm, meta_ref, count_ref,
+    ghosts, peers, target_ref, me_ref, source_ref, slot_ref, agg_ref, a_ref, p_ref, own_ref, sum_ref, tiles_hbm, meta_ref, count_ref,
     left_ref, first_ref, second_ref, odd_ref, even_tiles, odd_tiles, stage_ref,
     words_vec, words_ref, here_ref, done_ref, flying_ref, words_sem, sems,
 ):
@@ -129,20 +128,23 @@
     last = pl.num_programs(0) - 1
     per_row, rows = source_ref.shape
     pairs = (per_row + 3) // 4 * 2
-    sums = sum_ref.shape[0] // PIECES
+    sums = sum_ref.shape[0]
     low_half, low_all = lane_low(HALF), lane_low(B)
     zero_all = jnp.zeros((B, LANES), jnp.bfloat16)
 
     @pl.when(step == 0)
     def _():
         source, slot = source_ref[...], slot_ref[...]
-        part = (slot >= PS).astype(jnp.int32)
-        for i in range(2, PIECES):
-            part += (slot >= i * PS).astype(jnp.int32)
-        place = agg_ref[...] * PS + slot - part * PS
+        coarse_here = target_ref.shape[0]
+        agg = agg_ref[...]
+        near = jnp.zeros_like(agg)
+        for c in range(coarse_here):
+            peer = lax.rem(lax.div(target_ref[c], coarse_here), peers)
+            near = jnp.where(agg == c, ((peer ^ me_ref[0]) < peers // 2).astype(jnp.int32), near)
+        place = agg * S + slot
         ghost = (source >= rows).astype(jnp.int32)
-        words_vec[0] = ((part * sums + place) << SRC_BITS) + jnp.minimum(source, rows)
-        words_vec[1] = (ghost << FLAG_BIT) + (jnp.maximum(source - rows, 0) << PLACE_BITS) + place
+        words_vec[0] = (place << SRC_BITS) + jnp.minimum(source, rows)
+        words_vec[1] = (ghost << FLAG_BIT) + (near << FLAG_BIT - 1) + (jnp.maximum(source - rows, 0) << PLACE_BITS) + place
         load = pltpu.make_async_copy(words_vec, words_ref, words_sem)
         load.start()
         for i in range(PIECES):
@@ -164,9 +166,8 @@
         second_ref[rows] = zero_all
 
         def clear(i, carry):
-            for part in range(PIECES):
-                sum_ref[part * sums + i] = jnp.zeros((HALF, LANES), jnp.float32)
-                odd_ref[part * sums + i] = jnp.zeros((HALF, LANES), jnp.float32)
+            sum_ref[i] = jnp.zeros((HALF, LANES), jnp.float32)
+            odd_ref[i] = jnp.zeros((HALF, LANES), jnp.float32)
             return carry
 
         lax.fori_loop(0, sums, clear, 0, unroll=4)
@@ -208,11 +209,12 @@
                     halves.append(table[word & ((1 << SRC_BITS) - 1)])
                     targets.append(word >> SRC_BITS)
                     if k > 0:
-                        at = counts[parity]
                         note = words_ref[1, k, row]
+                        shift = (note >> FLAG_BIT - 4) & 8
+                        at = ((counts[parity] >> shift) & (LIST - 1)) + (shift << 4)
                         listed[at] = tile
                         here_ref[parity, at] = note
-                        counts[parity] = at + (note >> FLAG_BIT)
+                        counts[parity] += (note >> FLAG_BIT) << shift
                 filled = jnp.concatenate(halves, axis=0)
                 value = jnp.dot(tile, filled, preferred_element_type=jnp.float32)
                 even, odd = fold(value, low_half)
@@ -222,7 +224,8 @@
 
     no_entry = (ghosts << PLACE_BITS) + sums
     for part in range(PIECES):
-        even_count, odd_count = counts
+        even_count = (counts[0] >> 8 * part) & (LIST - 1)
+        odd_count = (counts[1] >> 8 * part) & (LIST - 1)
         after = jnp.maximum(even_count, odd_count)
         before = done_ref[part]
         chunks = lax.div(after + CHUNK - 1, CHUNK) + jnp.where(step == last, 1, 0)
@@ -266,8 +269,7 @@
     @pl.when(step == last)
     def _():
         def total(i, carry):
-            for part in range(PIECES):
-                sum_ref[part * sums + i] += odd_ref[part * sums + i]
+            sum_ref[i] += odd_ref[i]
             return carry
 
         lax.fori_loop(0, sums, total, 0, unroll=4)
@@ -285,22 +287,27 @@
             lax.fori_loop(0, flying_ref[part], drain, 0)
 
 
+def offsets_of(part, peers):
+    return range(peers // 2, peers) if part == 0 else range(peers // 2)
+
+
 def combine_kernel(
     part, peers, meta_ref, count_ref, target_ref, me_ref, ghost_hbm, sum_hbm, tiles_hbm, *rest
 ):
-    outs = rest[:peers]
+    mine = offsets_of(part, peers)
+    outs = dict(zip(mine, rest))
     (
         ghost_ref, even_ref, odd_ref, tiles_ref, out_ref, bucket_ref, place_ref, per_peer_ref,
         ghost_sem, sum_sem, note_sems, sems, out_sems,
-    ) = rest[peers:]
+    ) = rest[len(mine) :]
     me = me_ref[0]
     ghosts = ghost_hbm.shape[0]
     coarse_here = target_ref.shape[0]
-    sums = coarse_here * PS
+    sums = coarse_here * S
     chunks = count_ref[part]
     low_half = lane_low(HALF)
     zero_half = jnp.zeros((HALF, LANES), jnp.bfloat16)
-    load_sums = pltpu.make_async_copy(sum_hbm.at[pl.ds(part * sums, sums)], even_ref.at[pl.ds(0, sums)], sum_sem)
+    load_sums = pltpu.make_async_copy(sum_hbm, even_ref.at[pl.ds(0, sums)], sum_sem)
     load_sums.start()
     load_ghosts = pltpu.make_async_copy(ghost_hbm, ghost_ref.at[pl.ds(0, ghosts)], ghost_sem)
     load_ghosts.start()
@@ -338,7 +345,7 @@
         return carry
 
     lax.fori_loop(0, coarse_here, assign, 0)
-    payload = CCAP * PS * HALF
+    payload = CCAP * S * HALF
     second_slot = lax.broadcasted_iota(jnp.int32, (out_ref.shape[1] - payload, LANES), 1) // HALF % CCAP
 
     def note(p, carry):
@@ -354,7 +361,7 @@
     def put_notes(d):
         return pltpu.make_async_copy(out_ref.at[d, notes], outs[d].at[notes], note_sems.at[d])
 
-    for d in range(peers):
+    for d in mine:
         put_notes(d).start()
     load_ghosts.wait()
     load_sums.wait()
@@ -369,8 +376,8 @@
         for j in range(CHUNK):
             at = i * CHUNK + j
             even, odd = meta_ref[2 * part, at], meta_ref[2 * part + 1, at]
-            first = ghost_ref[(even >> PLACE_BITS) & ((1 << FLAG_BIT - PLACE_BITS) - 1)]
-            second = ghost_ref[(odd >> PLACE_BITS) & ((1 << FLAG_BIT - PLACE_BITS) - 1)]
+            first = ghost_ref[(even >> PLACE_BITS) & ((1 << FLAG_BIT - PLACE_BITS - 1) - 1)]
+            second = ghost_ref[(odd >> PLACE_BITS) & ((1 << FLAG_BIT - PLACE_BITS - 1) - 1)]
             filled = jnp.concatenate(
                 [
                     jnp.where(low_half, first, zero_half),
@@ -389,18 +396,22 @@
     lax.fori_loop(0, chunks, work, 0)
 
     def put(c, d, start):
-        span = pl.ds(start, PS * HALF)
+        span = pl.ds(start, S * HALF)
         return pltpu.make_async_copy(out_ref.at[d, span], outs[d].at[span], out_sems.at[c])
 
     def finish(c, carry):
         bucket = bucket_ref[c]
-        start = pl.multiple_of(lax.rem(bucket, CCAP) * (PS * HALF), HALF)
+        start = pl.multiple_of(lax.rem(bucket, CCAP) * (S * HALF), HALF)
         offset = lax.div(bucket, CCAP) ^ me
-        first = c * PS
-        for s in range(PS):
-            total = even_ref[first + s] + odd_ref[first + s]
-            out_ref[offset, pl.ds(pl.multiple_of(start + s * HALF, HALF), HALF)] = total.astype(jnp.bfloat16)
-        for d in range(peers):
+        first = c * S
+
+        @pl.when((offset >= mine[0]) & (offset <= mine[-1]))
+        def _():
+            for s in range(S):
+                total = even_ref[first + s] + odd_ref[first + s]
+                out_ref[offset, pl.ds(pl.multiple_of(start + s * HALF, HALF), HALF)] = total.astype(jnp.bfloat16)
+
+        for d in mine:
 
             @pl.when(offset == d)
             def _():
@@ -409,9 +420,19 @@
         return carry
 
     lax.fori_loop(0, coarse_here, finish, 0)
-    for d in range(peers):
+    for d in mine:
         put_notes(d).wait()
-    lax.fori_loop(0, coarse_here, lambda c, carry: (put(c, 0, 0).wait(), carry)[1], 0)
+
+    def drain(c, carry):
+        offset = lax.div(bucket_ref[c], CCAP) ^ me
+
+        @pl.when((offset >= mine[0]) & (offset <= mine[-1]))
+        def _():
+            put(c, mine[0], 0).wait()
+
+        return carry
+
+    lax.fori_loop(0, coarse_here, drain, 0)
 
 
 def place_kernel(peers, *refs):
@@ -419,22 +440,23 @@
     out_ref, in_ref, peer_ref, start_ref, sems = refs[peers:]
     step = pl.program_id(0)
     per_step, groups = out_ref.shape[0], out_ref.shape[1]
-    payload = CCAP * PS * HALF
+    payload = CCAP * S * HALF
 
     @pl.when(step == 0)
     def _():
         loads = [pltpu.make_async_copy(parts[d], in_ref.at[d], sems.at[d]) for d in range(peers)]
         for load in loads:
             load.start()
+        for load in loads:
+            load.wait()
         for p in range(peers):
-            loads[p].wait()
             notes = in_ref[p, payload:].astype(jnp.float32)
             which = lax.broadcasted_iota(jnp.int32, notes.shape, 1) // HALF
             for q in range(CCAP):
                 place = jnp.max(jnp.where(which == q, notes, -1.0)).astype(jnp.int32)
                 entry = jnp.where(place < 0, groups * GROUP, place)
                 peer_ref[entry] = p
-                start_ref[entry] = q * PS * HALF
+                start_ref[entry] = q * S * HALF
 
     perm = block_perm(True)
     low = lane_low(LANES)
@@ -499,12 +521,15 @@
         outgoing.reshape(peers, slots, HALF, LANES), ("px", "py"), split_axis=0, concat_axis=0, tiled=True
     ).reshape(peers * slots, HALF, LANES)
 
-    sums = coarse_here * PS
+    me = lax.axis_index("py").reshape(1)
+    sums = coarse_here * S
     room = groups * LIST + STAGE
     local, tiles, meta, count = pl.pallas_call(
-        functools.partial(project_kernel, peers * slots),
+        functools.partial(project_kernel, peers * slots, peers_y),
         grid=(groups,),
         in_specs=[
+            smem,
+            smem,
             whole((per_row, rows)),
             whole((per_row, rows)),
             whole((1, rows)),
@@ -512,9 +537,9 @@
             pl.BlockSpec((1, KROWS, LANES), lambda g: (g, 0, 0)),
             whole((rows, HALF, LANES)),
         ],
-        out_specs=[whole((PIECES * sums, HALF, LANES)), hbm, smem, smem],
+        out_specs=[whole((sums, HALF, LANES)), hbm, smem, smem],
         out_shape=[
-            jax.ShapeDtypeStruct((PIECES * sums, HALF, LANES), jnp.float32),
+            jax.ShapeDtypeStruct((sums, HALF, LANES), jnp.float32),
             jax.ShapeDtypeStruct((PIECES, room, B, LANES), bf16),
             jax.ShapeDtypeStruct((2 * PIECES, room), jnp.int32),
             jax.ShapeDtypeStruct((PIECES,), jnp.int32),
@@ -523,7 +548,7 @@
             pltpu.VMEM((GROUP * B, 2 * KROWS), bf16),
             pltpu.VMEM((rows + 1, B, LANES), bf16),
             pltpu.VMEM((rows + 1, B, LANES), bf16),
-            pltpu.VMEM((PIECES * sums, HALF, LANES), jnp.float32),
+            pltpu.VMEM((sums, HALF, LANES), jnp.float32),
             pltpu.VMEM((PIECES * LIST, B, LANES), bf16),
             pltpu.VMEM((PIECES * LIST, B, LANES), bf16),
             pltpu.VMEM((PIECES, STAGE, B, LANES), bf16),
@@ -539,36 +564,37 @@
         cost_estimate=pl.CostEstimate(
             flops=4 * 512 * 512 * 128 * pairs * groups, bytes_accessed=45_000_000, transcendentals=0
         ),
-    )(a_source.T, coarse_slot.T, agg_local.reshape(1, rows), a_tiles, p_tiles, own)
-
-    piece_rows = CCAP * PS * HALF + 16
-    me = lax.axis_index("py").reshape(1)
-    sent = pl.pallas_call(
-        functools.partial(combine_kernel, 0, peers_y),
-        in_specs=[smem, smem, smem, smem, hbm, hbm, hbm],
-        out_specs=[hbm] * peers_y,
-        out_shape=[jax.ShapeDtypeStruct((piece_rows, LANES), bf16)] * peers_y,
-        scratch_shapes=[
-            pltpu.VMEM((peers * slots + 1, HALF, LANES), bf16),
-            pltpu.VMEM((sums + 1, HALF, LANES), jnp.float32),
-            pltpu.VMEM((sums + 1, HALF, LANES), jnp.float32),
-            pltpu.VMEM((RING, CHUNK, B, LANES), bf16),
-            pltpu.VMEM((peers_y, piece_rows, LANES), bf16),
-            pltpu.SMEM((coarse_here,), jnp.int32),
-            pltpu.SMEM((peers_y * CCAP,), jnp.int32),
-            pltpu.SMEM((peers_y,), jnp.int32),
-            pltpu.SemaphoreType.DMA,
-            pltpu.SemaphoreType.DMA,
-            pltpu.SemaphoreType.DMA((peers_y,)),
-            pltpu.SemaphoreType.DMA((RING,)),
-            pltpu.SemaphoreType.DMA((coarse_here,)),
-        ],
-        compiler_params=pltpu.CompilerParams(vmem_limit_bytes=56 * MIB),
-        cost_estimate=pl.CostEstimate(flops=4_000_000_000, bytes_accessed=8_000_000, transcendentals=0),
-    )(meta, count, coarse_target, me, arrived, local, tiles)
-    received = [sent[0]]
-    for d in range(1, peers_y):
-        received.append(lax.ppermute(sent[d], "py", [(i, i ^ d) for i in range(peers_y)]))
+    )(coarse_target, me, a_source.T, coarse_slot.T, agg_local.reshape(1, rows), a_tiles, p_tiles, own)
+
+    piece_rows = CCAP * S * HALF + 16
+    received = [None] * peers_y
+    for part in range(PIECES):
+        sent = pl.pallas_call(
+            functools.partial(combine_kernel, part, peers_y),
+            in_specs=[smem, smem, smem, smem, hbm, hbm, hbm],
+            out_specs=[hbm] * len(offsets_of(part, peers_y)),
+            out_shape=[jax.ShapeDtypeStruct((piece_rows, LANES), bf16)] * len(offsets_of(part, peers_y)),
+            scratch_shapes=[
+                pltpu.VMEM((peers * slots + 1, HALF, LANES), bf16),
+                pltpu.VMEM((sums + 1, HALF, LANES), jnp.float32),
+                pltpu.VMEM((sums + 1, HALF, LANES), jnp.float32),
+                pltpu.VMEM((RING, CHUNK, B, LANES), bf16),
+                pltpu.VMEM((peers_y, piece_rows, LANES), bf16),
+                pltpu.SMEM((coarse_here,), jnp.int32),
+                pltpu.SMEM((peers_y * CCAP,), jnp.int32),
+                pltpu.SMEM((peers_y,), jnp.int32),
+                pltpu.SemaphoreType.DMA,
+                pltpu.SemaphoreType.DMA,
+                pltpu.SemaphoreType.DMA((peers_y,)),
+                pltpu.SemaphoreType.DMA((RING,)),
+                pltpu.SemaphoreType.DMA((coarse_here,)),
+            ],
+            compiler_params=pltpu.CompilerParams(vmem_limit_bytes=56 * MIB),
+            cost_estimate=pl.CostEstimate(flops=4_000_000_000, bytes_accessed=8_000_000, transcendentals=0),
+        )(meta, count, coarse_target, me, arrived, local, tiles)
+        for d, rows_out in zip(offsets_of(part, peers_y), sent):
+            pairs_of = [(i, i ^ d) for i in range(peers_y)]
+            received[d] = lax.ppermute(rows_out, "py", pairs_of) if d else rows_out
 
     per_step = 9
     out_groups = coarse_here // GROUP
@@ -584,7 +610,7 @@
             pltpu.SMEM((coarse_here + 1,), jnp.int32),
             pltpu.SemaphoreType.DMA((peers_y,)),
         ],
-        compiler_params=pltpu.CompilerParams(vmem_limit_bytes=24 * MIB),
+        compiler_params=pltpu.CompilerParams(vmem_limit_bytes=60 * MIB),
         cost_estimate=pl.CostEstimate(flops=1_000_000_000, bytes_accessed=3_000_000, transcendentals=0),
     )(*received)
     return from_tiles(placed).transpose(1, 0, 2)

time: 127 us -> 130 us (1.024)
  Pallas kernels: 68.9 us -> 79.3 us
  waiting for transfers between devices: 42.5 us -> 33.8 us
  starting transfers between devices: 14.2 us -> 16 us
    pallas_call x2 -> x3, Pallas kernels: 57.8 us -> 69.6 us  [the longest x1 47.6 us: body(): pl.pallas_call(functools.partial(project_kernel, peers * slots, peers_y),...]
    all_to_all x1, waiting for transfers between devices: 6.48 us -> 1.21 us  [body(): lax.all_to_all(outgoing.reshape(peers, slots, HALF, LANES), ('px', 'py'),...]
    ppermute x7, waiting for transfers between devices: 36 us -> 32.6 us  [body(): received[d] = lax.ppermute(rows_out, 'py', pairs_of) if d else rows_out]
    ppermute x7, starting transfers between devices: 6.78 us -> 8.52 us  [body(): received[d] = lax.ppermute(rows_out, 'py', pairs_of) if d else rows_out]
    pallas_call x1, Pallas kernels: 6.73 us -> 5.41 us  [body(): pl.pallas_call(functools.partial(place_kernel, peers_y), grid=(S // per_s...]
  transfers between devices with their start and end apart: 8 -> 8, of which waited for: 4 -> 5; matrix products, arithmetic and copies ran while one was open for 0% -> 0% of each run, Pallas kernels for 33% -> 45%
where the time goes in v6:
time: 130 us
  Pallas kernels  79.3 us (61%)
  waiting for transfers between devices  33.8 us (26%)
  starting transfers between devices  16 us (12%)
    pallas_call x1, Pallas kernels, body(): pl.pallas_call(functools.partial(project_kernel, peers * slots, peers_y),...  47.6 us
    ppermute x7, waiting for transfers between devices, body(): received[d] = lax.ppermute(rows_out, 'py', pairs_of) if d else rows_out  32.6 us
    pallas_call x2, Pallas kernels, body(): pl.pallas_call(functools.partial(combine_kernel, part, peers_y), in_specs...  22 us
    ppermute x7, starting transfers between devices, body(): received[d] = lax.ppermute(rows_out, 'py', pairs_of) if d else rows_out  8.52 us
    all_to_all x1, starting transfers between devices, body(): lax.all_to_all(outgoing.reshape(peers, slots, HALF, LANES), ('px', 'py'),...  7.43 us
    pallas_call x1, Pallas kernels, body(): pl.pallas_call(functools.partial(place_kernel, peers_y), grid=(S // per_s...  5.41 us
    pallas_call x1, Pallas kernels, body(): pl.pallas_call(pack_kernel, in_specs=[hbm, hbm], out_specs=[hbm, hbm], ou...  4.31 us
  transfers between devices with their start and end apart: 8, of which 5 were waited for; matrix products, arithmetic and copies ran while one was open for 0% of the time, Pallas kernels for 45%

profile of v6, /device:TPU:0, one launch (start us, length us, event | category | flops | bytes accessed | tf_op | source)
XLA Modules:
  0.0 129.9 jit_solution(464862737782137186)
XLA Ops:
  0.0 4.3 %shard_map.73 = (bf16[256,32,128]{2,1,0:T(8,128)(2,1)}, bf16[96,32,128]{2,1,0:T(8,128)(2,1)}) custom-call(s32[8,32]{1,0:T(8,128)} %bitcast.31, bf16[12,256,128]{2,1,0:T(8,128)(2,1)} %bitcast.29), custom_call_target="tpu_custom_call" | custom-call | tf_op jit(solution)/shard_map/pallas_call | solution.py:500
  4.3 7.4 %all-to-all-start = ((bf16[32,8,32,128]{3,2,1,0:T(8,128)(2,1)}), bf16[32,8,32,128]{3,2,1,0:T(8,128)(2,1)}, u32[]{:S(2)}, u32[]{:S(2)}) async-start(bf16[32,8,32,128]{3,2,1,0:T(8,128)(2,1)} %bitcast.28), calls=%async_computation | async-start | bytes 4194304 | tf_op jit(solution)/shard_map/all_to_all | solution.py:520
  11.8 47.6 %shard_map.74 = (f32[432,32,128]{2,1,0:T(8,128)}, bf16[2,1728,64,128]{3,2,1,0:T(8,128)(2,1)}, s32[4,1728]{1,0:T(4,128)}, s32[2]{0:T(128)}) custom-call(s32[16]{0:T(128)} %target_ref.5, s32[1]{0:T(128)} %bitcast.me_ref, s32[27,96]{1,0:T(8,128)} %bitcast.33, s32[27,96]{1,0:T(8,128)} %bitcast.34, s32[1,96]{1,0:T(1,128)} %bitcast.35, ...), custom_call_target="tpu_custom_call" | custom-call | flops 22548578304 | bytes 45000000 | tf_op jit(solution)/shard_map/pallas_call | solution.py:527
  59.4 1.2 all-to-all-done
  60.6 10.9 %shard_map.76 = (bf16[1744,128]{1,0:T(8,128)(2,1)}, bf16[1744,128]{1,0:T(8,128)(2,1)}, bf16[1744,128]{1,0:T(8,128)(2,1)}, bf16[1744,128]{1,0:T(8,128)(2,1)}) custom-call(s32[4,1728]{1,0:T(4,128)} %get-tuple-element.20.meta_ref, s32[2]{0:T(128)} %get-tuple-element.21.count_ref, s32[16]{0:T(128)} %target_ref.5, s32[1]{0:T(128)} %bitcast.me_ref, ...), custom_call_target="tpu_custom_call" | custom-call | flops 4000000000 | bytes 8000000 | tf_op jit(solution)/shard_map/pallas_call | solution.py:572
  71.6 1.4 %collective-permute-start.3 = (bf16[1744,128]{1,0:T(8,128)(2,1)}, bf16[1744,128]{1,0:T(8,128)(2,1)S(1)}, u32[]{:S(2)}, u32[]{:S(2)}) collective-permute-start(bf16[1744,128]{1,0:T(8,128)(2,1)} %get-tuple-element.29), channel_id=1, source_target_pairs={{0,4},{1,5},{2,6},{3,7},{4,0},{5,1},{6,2},{7,3},{8,12},{9,13},{10,... | collective-permute-start | bytes 1339400 | tf_op jit(solution)/shard_map/ppermute | solution.py:597
  72.9 0.0 collective-permute-start.4
  72.9 1.9 %collective-permute-start.5 = (bf16[1744,128]{1,0:T(8,128)(2,1)}, bf16[1744,128]{1,0:T(8,128)(2,1)S(1)}, u32[]{:S(2)}, u32[]{:S(2)}) collective-permute-start(bf16[1744,128]{1,0:T(8,128)(2,1)} %get-tuple-element.31), channel_id=1, source_target_pairs={{0,6},{1,7},{2,4},{3,5},{4,2},{5,3},{6,0},{7,1},{8,14},{9,15},{10,... | collective-permute-start | bytes 1339400 | tf_op jit(solution)/shard_map/ppermute | solution.py:597
  74.8 1.2 collective-permute-start.6
  76.0 11.0 %shard_map.75 = (bf16[1744,128]{1,0:T(8,128)(2,1)}, bf16[1744,128]{1,0:T(8,128)(2,1)}, bf16[1744,128]{1,0:T(8,128)(2,1)}, bf16[1744,128]{1,0:T(8,128)(2,1)}) custom-call(s32[4,1728]{1,0:T(4,128)} %get-tuple-element.20.meta_ref, s32[2]{0:T(128)} %get-tuple-element.21.count_ref, s32[16]{0:T(128)} %target_ref.5, s32[1]{0:T(128)} %bitcast.me_ref, ...), custom_call_target="tpu_custom_call" | custom-call | flops 4000000000 | bytes 8000000 | tf_op jit(solution)/shard_map/pallas_call | solution.py:572
  87.1 0.1 collective-permute-start
  87.2 17.0 %collective-permute-done.3.refs_4_ = bf16[1744,128]{1,0:T(8,128)(2,1)S(1)} collective-permute-done((bf16[1744,128]{1,0:T(8,128)(2,1)}, bf16[1744,128]{1,0:T(8,128)(2,1)S(1)}, u32[]{:S(2)}, u32[]{:S(2)}) %collective-permute-start.3) | collective-permute-done | bytes 446496 | tf_op jit(solution)/shard_map/ppermute | solution.py:597
  104.2 0.0 copy-start
  104.2 1.4 %collective-permute-start.1 = (bf16[1744,128]{1,0:T(8,128)(2,1)}, bf16[1744,128]{1,0:T(8,128)(2,1)S(1)}, u32[]{:S(2)}, u32[]{:S(2)}) collective-permute-start(bf16[1744,128]{1,0:T(8,128)(2,1)} %get-tuple-element.27), channel_id=1, source_target_pairs={{0,2},{1,3},{2,0},{3,1},{4,6},{5,7},{6,4},{7,5},{8,10},{9,11},{10,... | collective-permute-start | bytes 1339400 | tf_op jit(solution)/shard_map/ppermute | solution.py:597
  105.6 5.4 %collective-permute-done.4.refs_5_ = bf16[1744,128]{1,0:T(8,128)(2,1)S(1)} collective-permute-done((bf16[1744,128]{1,0:T(8,128)(2,1)}, bf16[1744,128]{1,0:T(8,128)(2,1)S(1)}, u32[]{:S(2)}, u32[]{:S(2)}) %collective-permute-start.4) | collective-permute-done | bytes 446496 | tf_op jit(solution)/shard_map/ppermute | solution.py:597
  111.0 0.0 copy-start.1
  111.0 2.6 %collective-permute-start.2 = (bf16[1744,128]{1,0:T(8,128)(2,1)}, bf16[1744,128]{1,0:T(8,128)(2,1)S(1)}, u32[]{:S(2)}, u32[]{:S(2)}) collective-permute-start(bf16[1744,128]{1,0:T(8,128)(2,1)} %get-tuple-element.28), channel_id=1, source_target_pairs={{0,3},{1,2},{2,1},{3,0},{4,7},{5,6},{6,5},{7,4},{8,11},{9,10},{10,... | collective-permute-start | bytes 1339400 | tf_op jit(solution)/shard_map/ppermute | solution.py:597
  113.6 0.0 collective-permute-done.5.refs_6_
  113.6 0.0 copy-start.2
  113.6 0.0 collective-permute-done.6.refs_7_
  113.6 0.0 copy-start.3
  113.6 0.0 collective-permute-done.refs_1_
  113.6 0.0 copy-start.4
  113.6 0.3 collective-permute-done.1.refs_2_
  113.9 0.0 copy-start.5
  113.9 9.8 %collective-permute-done.2.refs_3_ = bf16[1744,128]{1,0:T(8,128)(2,1)S(1)} collective-permute-done((bf16[1744,128]{1,0:T(8,128)(2,1)}, bf16[1744,128]{1,0:T(8,128)(2,1)S(1)}, u32[]{:S(2)}, u32[]{:S(2)}) %collective-permute-start.2) | collective-permute-done | bytes 446496 | tf_op jit(solution)/shard_map/ppermute | solution.py:597
  123.7 0.0 copy-start.6
  123.8 0.0 copy-done
  123.8 0.0 copy-done.1
  123.8 0.0 copy-done.2
  123.8 0.0 copy-done.3
  123.8 0.0 copy-done.4
  123.8 0.0 copy-done.5
  123.8 0.7 copy-done.6
  124.5 5.4 %shard_map.77 = bf16[27,2,256,128]{3,2,1,0:T(8,128)(2,1)} custom-call(bf16[1744,128]{1,0:T(8,128)(2,1)} %get-tuple-element.25.refs_0_, bf16[1744,128]{1,0:T(8,128)(2,1)} %copy-done.4, bf16[1744,128]{1,0:T(8,128)(2,1)} %copy-done.5, bf16[1744,128]{1,0:T(8,128)(2,1)} %copy-done.6, bf16[1744,128]{1,0:T(8,128)(2,1)} %copy-done, bf16[1744,128]{1,0:T(8,128)(2,1)} %copy-done.1, ...), custom_call_target="tpu_custom_call" | custom-call | flops 1000000000 | bytes 3000000 | tf_op jit(solution)/shard_map/pallas_call | solution.py:601
Async XLA Ops:
  4.3 56.3 %all-to-all-start = ((bf16[32,8,32,128]{3,2,1,0:T(8,128)(2,1)}), bf16[32,8,32,128]{3,2,1,0:T(8,128)(2,1)}, u32[]{:S(2)}, u32[]{:S(2)}) async-start(bf16[32,8,32,128]{3,2,1,0:T(8,128)(2,1)} %bitcast.28), calls=%async_computation | async-start | bytes 4194304 | tf_op jit(solution)/shard_map/all_to_all | solution.py:520
  71.6 32.6 %collective-permute-start.3 = (bf16[1744,128]{1,0:T(8,128)(2,1)}, bf16[1744,128]{1,0:T(8,128)(2,1)S(1)}, u32[]{:S(2)}, u32[]{:S(2)}) collective-permute-start(bf16[1744,128]{1,0:T(8,128)(2,1)} %get-tuple-element.29), channel_id=1, source_target_pairs={{0,4},{1,5},{2,6},{3,7},{4,0},{5,1},{6,2},{7,3},{8,12},{9,13},{10,... | collective-permute-start | bytes 1339400 | tf_op jit(solution)/shard_map/ppermute | solution.py:597
  72.9 38.1 %collective-permute-start.4 = (bf16[1744,128]{1,0:T(8,128)(2,1)}, bf16[1744,128]{1,0:T(8,128)(2,1)S(1)}, u32[]{:S(2)}, u32[]{:S(2)}) collective-permute-start(bf16[1744,128]{1,0:T(8,128)(2,1)} %get-tuple-element.30), channel_id=1, source_target_pairs={{0,5},{1,4},{2,7},{3,6},{4,1},{5,0},{6,3},{7,2},{8,13},{9,12},{10,... | collective-permute-start | bytes 1339400 | tf_op jit(solution)/shard_map/ppermute | solution.py:597
  72.9 40.6 %collective-permute-start.5 = (bf16[1744,128]{1,0:T(8,128)(2,1)}, bf16[1744,128]{1,0:T(8,128)(2,1)S(1)}, u32[]{:S(2)}, u32[]{:S(2)}) collective-permute-start(bf16[1744,128]{1,0:T(8,128)(2,1)} %get-tuple-element.31), channel_id=1, source_target_pairs={{0,6},{1,7},{2,4},{3,5},{4,2},{5,3},{6,0},{7,1},{8,14},{9,15},{10,... | collective-permute-start | bytes 1339400 | tf_op jit(solution)/shard_map/ppermute | solution.py:597
  74.8 38.8 %collective-permute-start.6 = (bf16[1744,128]{1,0:T(8,128)(2,1)}, bf16[1744,128]{1,0:T(8,128)(2,1)S(1)}, u32[]{:S(2)}, u32[]{:S(2)}) collective-permute-start(bf16[1744,128]{1,0:T(8,128)(2,1)} %get-tuple-element.32), channel_id=1, source_target_pairs={{0,7},{1,6},{2,5},{3,4},{4,3},{5,2},{6,1},{7,0},{8,15},{9,14},{10,... | collective-permute-start | bytes 1339400 | tf_op jit(solution)/shard_map/ppermute | solution.py:597
  87.1 26.5 %collective-permute-start = (bf16[1744,128]{1,0:T(8,128)(2,1)}, bf16[1744,128]{1,0:T(8,128)(2,1)S(1)}, u32[]{:S(2)}, u32[]{:S(2)}) collective-permute-start(bf16[1744,128]{1,0:T(8,128)(2,1)} %get-tuple-element.26), channel_id=1, source_target_pairs={{0,1},{1,0},{2,3},{3,2},{4,5},{5,4},{6,7},{7,6},{8,9},{9,8},{10,11... | collective-permute-start | bytes 1339400 | tf_op jit(solution)/shard_map/ppermute | solution.py:597
  104.2 19.6 %copy-start = (bf16[1744,128]{1,0:T(8,128)(2,1)}, bf16[1744,128]{1,0:T(8,128)(2,1)S(1)}, u32[]{:S(2)}) copy-start(bf16[1744,128]{1,0:T(8,128)(2,1)S(1)} %collective-permute-done.3.refs_4_) | copy-start | bytes 1339396
  104.2 9.8 %collective-permute-start.1 = (bf16[1744,128]{1,0:T(8,128)(2,1)}, bf16[1744,128]{1,0:T(8,128)(2,1)S(1)}, u32[]{:S(2)}, u32[]{:S(2)}) collective-permute-start(bf16[1744,128]{1,0:T(8,128)(2,1)} %get-tuple-element.27), channel_id=1, source_target_pairs={{0,2},{1,3},{2,0},{3,1},{4,6},{5,7},{6,4},{7,5},{8,10},{9,11},{10,... | collective-permute-start | bytes 1339400 | tf_op jit(solution)/shard_map/ppermute | solution.py:597
  111.0 12.8 %copy-start.1 = (bf16[1744,128]{1,0:T(8,128)(2,1)}, bf16[1744,128]{1,0:T(8,128)(2,1)S(1)}, u32[]{:S(2)}) copy-start(bf16[1744,128]{1,0:T(8,128)(2,1)S(1)} %collective-permute-done.4.refs_5_) | copy-start | bytes 1339396
  111.0 12.8 %collective-permute-start.2 = (bf16[1744,128]{1,0:T(8,128)(2,1)}, bf16[1744,128]{1,0:T(8,128)(2,1)S(1)}, u32[]{:S(2)}, u32[]{:S(2)}) collective-permute-start(bf16[1744,128]{1,0:T(8,128)(2,1)} %get-tuple-element.28), channel_id=1, source_target_pairs={{0,3},{1,2},{2,1},{3,0},{4,7},{5,6},{6,5},{7,4},{8,11},{9,10},{10,... | collective-permute-start | bytes 1339400 | tf_op jit(solution)/shard_map/ppermute | solution.py:597
  113.6 10.2 %copy-start.2 = (bf16[1744,128]{1,0:T(8,128)(2,1)}, bf16[1744,128]{1,0:T(8,128)(2,1)S(1)}, u32[]{:S(2)}) copy-start(bf16[1744,128]{1,0:T(8,128)(2,1)S(1)} %collective-permute-done.5.refs_6_) | copy-start | bytes 1339396
  113.6 10.2 %copy-start.3 = (bf16[1744,128]{1,0:T(8,128)(2,1)}, bf16[1744,128]{1,0:T(8,128)(2,1)S(1)}, u32[]{:S(2)}) copy-start(bf16[1744,128]{1,0:T(8,128)(2,1)S(1)} %collective-permute-done.6.refs_7_) | copy-start | bytes 1339396
  113.6 10.2 %copy-start.4 = (bf16[1744,128]{1,0:T(8,128)(2,1)}, bf16[1744,128]{1,0:T(8,128)(2,1)S(1)}, u32[]{:S(2)}) copy-start(bf16[1744,128]{1,0:T(8,128)(2,1)S(1)} %collective-permute-done.refs_1_) | copy-start | bytes 1339396
  113.9 9.9 %copy-start.5 = (bf16[1744,128]{1,0:T(8,128)(2,1)}, bf16[1744,128]{1,0:T(8,128)(2,1)S(1)}, u32[]{:S(2)}) copy-start(bf16[1744,128]{1,0:T(8,128)(2,1)S(1)} %collective-permute-done.1.refs_2_) | copy-start | bytes 1339396
  123.7 0.8 copy-start.6
